TPU v7x, 32 devices: a whole 2x2x4 slice. The times are simulated.
32 devices in a mesh: grp: 2 (over x), tp: 16 (over z, y, core).
Axes of the slice: x: 2, y: 2, z: 4, core: 2. Of those that a mesh axis runs over, the one named last changes fastest.
Arguments:
- queries: bfloat16 [256, 128, 576], P(('grp', 'tp'))
- kv_cache: bfloat16 [256, 512, 576], P(('grp', 'tp'))
- lengths: int32 [256], P(('grp', 'tp')), may hold values from 1 to 512, as said below
- residual: bfloat16 [256, 7168], P(('grp', 'tp')), may hold values from -6 to 6
- uv_weight: bfloat16 [128, 512, 128], P('tp'), may hold values from -1 to 1
- out_weight: bfloat16 [16384, 7168], P('tp'), may hold values from -0.1875 to 0.1875
- expert_ids: int32 [256, 8], P(('grp', 'tp')), may hold values from 0 to 15, all different within a row; in each aligned block of 8 rows (0 to 7, 8 to 15, ...) at most 8 rows name the same one
- gate_values: bfloat16 [256, 8], P(('grp', 'tp')), may hold values from 0.099609375 to 0.59765625
- w_gate: bfloat16 [16, 7168, 512], P('tp', None, 'grp'), may hold values from -0.0625 to 0.0625
- w_up: bfloat16 [16, 7168, 512], P('tp', None, 'grp'), may hold values from -0.0625 to 0.0625
- w_down: bfloat16 [16, 512, 7168], P('tp', 'grp'), may hold values from -0.25 to 0.25
Outputs:
- mixed: bfloat16 [256, 7168], P(('grp', 'tp'))
Inputs may be any that keep to these rules, and one draw needn't show every extreme that they name: `lengths`: every row has at least one live position; in every draw some row has all 512 live. `expert_ids`: A row's 8 experts are distinct. Among the 8 rows of one device no expert is chosen more than 8 times, and in every draw some device reaches that count.
All inputs are finite; a program needn't handle non-finite values.
Results may differ from a plain program's by a relative error of at most 0.015.
Values may be sent and summed in bfloat16 or wider, within the bound.
A program may use at most 128 MiB of HBM per device.

v0:
```python
import jax
import jax.numpy as jnp
from jax import lax
from jax.sharding import PartitionSpec as P


def body(
    queries,
    kv_cache,
    lengths,
    residual,
    uv_weight,
    out_weight,
    expert_ids,
    gate_values,
    w_gate,
    w_up,
    w_down,
):
    rows_here = residual.shape[0]
    latent = uv_weight.shape[1]
    width = residual.shape[1]
    span = kv_cache.shape[1]
    scores = jnp.einsum(
        "rhc,rlc->rhl", queries, kv_cache, preferred_element_type=jnp.float32
    ) * queries.shape[2] ** (-0.5)
    valid = lax.broadcasted_iota(jnp.int32, (1, 1, span), 2) < lengths[:, None, None]
    top = jnp.max(jnp.where(valid, scores, -jnp.inf), axis=-1, keepdims=True)
    expo = jnp.where(valid, jnp.exp(scores - top), 0.0)
    probs = (expo / jnp.sum(expo, axis=-1, keepdims=True)).astype(jnp.bfloat16)
    context = jnp.einsum(
        "rhl,rlc->rhc", probs, kv_cache[:, :, :latent], preferred_element_type=jnp.float32
    ).astype(jnp.bfloat16)
    grouped = lax.all_to_all(context, "tp", split_axis=1, concat_axis=0, tiled=True)
    values = jnp.einsum(
        "rhc,hcv->rhv", grouped, uv_weight, preferred_element_type=jnp.float32
    ).astype(jnp.bfloat16)
    values = values.reshape(values.shape[0], values.shape[1] * values.shape[2])
    attention = lax.psum_scatter(
        jnp.dot(values, out_weight, preferred_element_type=jnp.float32).astype(jnp.bfloat16),
        "tp",
        scatter_dimension=0,
        tiled=True,
    ).astype(jnp.float32)
    hidden_state = residual.astype(jnp.float32) + attention
    normed = (
        hidden_state
        * lax.rsqrt(jnp.mean(hidden_state * hidden_state, axis=-1, keepdims=True) + 1e-06)
    ).astype(jnp.bfloat16)
    experts = lax.axis_size("tp")
    groups = lax.axis_size("grp")
    topk = expert_ids.shape[1]
    slots = 2 * rows_here * topk // experts
    flat = expert_ids.reshape(-1)
    picks = (flat[:, None] == lax.broadcasted_iota(jnp.int32, (1, experts), 1)).astype(jnp.int32)
    before = jnp.cumsum(picks, axis=0) - picks
    position = jnp.sum(before * picks, axis=1)
    expert_hot = picks.astype(jnp.float32).reshape(rows_here, topk, experts)
    slot_hot = (
        (position[:, None] == lax.broadcasted_iota(jnp.int32, (1, slots), 1))
        .astype(jnp.float32)
        .reshape(rows_here, topk, slots)
    )
    combine = jnp.einsum(
        "rk,rke,rkc->rec",
        gate_values.astype(jnp.float32),
        expert_hot,
        slot_hot,
        precision=lax.Precision.HIGHEST,
    )
    rows_all, combine_all = (
        lax.all_gather(normed, "grp", axis=0, tiled=True),
        lax.all_gather(combine.astype(jnp.bfloat16), "grp", axis=0, tiled=True),
    )
    combine_all = combine_all.reshape(groups, rows_here, experts, slots)
    dispatch_all = (combine_all > 0).astype(jnp.bfloat16)
    buffer = jnp.einsum(
        "jrec,jrd->ejcd",
        dispatch_all,
        rows_all.reshape(groups, rows_here, width),
        preferred_element_type=jnp.float32,
    )
    buffer = buffer.astype(jnp.bfloat16).reshape(experts * groups * slots, width)
    arrived = lax.all_to_all(buffer, "tp", split_axis=0, concat_axis=0, tiled=True)
    gate = jnp.dot(arrived, w_gate[0], preferred_element_type=jnp.float32)
    up = jnp.dot(arrived, w_up[0], preferred_element_type=jnp.float32)
    hidden = (jax.nn.silu(gate) * up).astype(jnp.bfloat16)
    partial_value = jnp.dot(hidden, w_down[0], preferred_element_type=jnp.float32)
    back = (
        lax.all_to_all(
            partial_value.astype(jnp.bfloat16), "tp", split_axis=0, concat_axis=0, tiled=True
        )
        .astype(partial_value.dtype)
        .reshape(experts, groups, slots, width)
    )
    terms = jnp.einsum(
        "jrec,ejcd->jrd", combine_all.astype(jnp.float32), back, precision=lax.Precision.HIGHEST
    )
    routed = lax.psum_scatter(
        terms.reshape(groups * rows_here, width).astype(jnp.bfloat16),
        "grp",
        scatter_dimension=0,
        tiled=True,
    ).astype(jnp.float32)
    return (hidden_state + routed).astype(jnp.bfloat16)


def solution(mesh):
    placed = (
        P(("grp", "tp"), None, None),
        P(("grp", "tp"), None, None),
        P(("grp", "tp")),
        P(("grp", "tp"), None),
        P("tp", None, None),
        P("tp", None),
        P(("grp", "tp"), None),
        P(("grp", "tp"), None),
        P("tp", None, "grp"),
        P("tp", None, "grp"),
        P("tp", "grp", None),
    )
    return jax.shard_map(
        body, mesh=mesh, in_specs=placed, out_specs=P(("grp", "tp"), None), check_vma=False
    )
```

profile of v0, /device:TPU:0, one launch (start us, length us, event | category | flops | bytes accessed | tf_op | source)
XLA Modules:
  0.0 334.7 jit_solution(1747704488084349514)
XLA Ops:
  6.5 0.8 iota_compare_fusion.5
  7.4 0.5 copy-done
  7.8 6.0 %fusion.55 = (f32[8,128]{1,0:T(8,128)S(1)}, f32[8,128,512]{2,1,0:T(8,128)S(1)}) fusion(pred[8,512]{1,0:T(8,128)(4,1)S(1)} %iota_compare_fusion.5, bf16[8,128,576]{1,2,0:T(8,128)(2,1)S(1)} %copy-done, bf16[8,512,576]{1,2,0:T(8,128)(2,1)} %param.12), kind=kOutput, calls=%fused_computation.64 | convolution fusion | flops 1211105792 | bytes 8003584 | tf_op jit(solution)/shard_map/sub | solution.py:29
  13.8 3.9 %fusion.14 = bf16[8,128,512]{2,1,0:T(8,128)(2,1)S(1)} fusion(bf16[8,512,576]{1,2,0:T(8,128)(2,1)} %param.12, f32[8,128,512]{2,1,0:T(8,128)S(1)} %get-tuple-element.6, f32[8,128]{1,0:T(8,128)S(1)} %get-tuple-element.5), kind=kOutput, calls=%fused_computation.19 | convolution fusion | flops 538443776 | bytes 7344128 | tf_op jit(solution)/shard_map/rhl,rlc->rhc/dot_general | solution.py:31
  17.7 0.6 copy.32
  18.3 32.3 %all_to_all.39 = bf16[8,128,512]{2,0,1:T(8,128)(2,1)S(1)} all-to-all(bf16[8,128,512]{2,0,1:T(8,128)(2,1)S(1)} %copy.32), channel_id=1, replica_groups=mesh['grp'=2,'tp'=16] {'tp'}, dimensions={1} | all-to-all | bytes 2097152 | tf_op jit(solution)/shard_map/all_to_all | solution.py:34
  50.6 0.5 convolution_convert_fusion.3
  51.1 3.7 %convolution_convert_fusion.2 = bf16[128,7168]{1,0:T(8,128)(2,1)} fusion(bf16[128,1024]{0,1:T(8,128)(2,1)S(1)} %bitcast.63, bf16[1024,7168]{1,0:T(8,128)(2,1)S(1)} %copy-done.1), kind=kOutput, calls=%fused_computation.3 | convolution fusion | flops 1879965696 | bytes 16777216 | tf_op jit(solution)/shard_map/dot_general | solution.py:40
  55.7 4.4 %all_gather.6 = bf16[16,16,8]{1,2,0:T(8,128)(2,1)S(1)} all-gather(bf16[8,16,8]{1,2,0:T(8,128)(2,1)S(1)} %convolution_convert_fusion.4), channel_id=1, replica_groups=mesh['grp'=2,'tp'=16] {'grp'}, dimensions={0}, use_global_device_ids=true | all-gather | bytes 6144 | tf_op jit(solution)/shard_map/all_gather | solution.py:73
  60.1 55.7 %reduce-scatter.3.cloned.1.call-done = bf16[8,7168]{1,0:T(8,128)(2,1)} async-done(((bf16[128,7168]{1,0:T(8,128)(2,1)}), bf16[8,7168]{1,0:T(8,128)(2,1)}) %reduce-scatter.3.cloned.1.call-update) | async-done | bytes 114704 | tf_op jit(solution)/shard_map/reduce_scatter | solution.py:39
  115.8 1.1 multiply_reduce_fusion
  116.9 1.0 multiply_convert_fusion
  117.9 5.5 %all_gather.7 = bf16[16,7168]{1,0:T(8,128)(2,1)S(1)} all-gather(bf16[8,7168]{1,0:T(8,128)(2,1)S(1)} %multiply_convert_fusion), channel_id=1, replica_groups=mesh['grp'=2,'tp'=16] {'grp'}, dimensions={0}, use_global_device_ids=true | all-gather | bytes 344064 | tf_op jit(solution)/shard_map/all_gather | solution.py:72
  123.4 1.1 convolution_convert_fusion.1
  124.5 2.0 copy.36
  126.5 84.8 %all_to_all.40 = bf16[16,16,7168]{2,1,0:T(8,128)(2,1)S(1)} all-to-all(bf16[16,16,7168]{2,1,0:T(8,128)(2,1)S(1)} %copy.36), channel_id=1, replica_groups=mesh['grp'=2,'tp'=16] {'tp'}, dimensions={0} | all-to-all | bytes 7340032 | tf_op jit(solution)/shard_map/all_to_all | solution.py:84
  211.3 1.8 copy-done.2
  213.1 1.1 fusion.8
  214.2 10.0 %convolution_convert_fusion = bf16[256,7168]{1,0:T(8,128)(2,1)} fusion(bf16[1,256,7168]{2,1,0:T(8,128)(2,1)} %param.21, bf16[256,7168]{1,0:T(8,128)(2,1)} %bitcast.58, bf16[1,7168,256]{2,1,0:T(8,128)(2,1)} %param.20, f32[256,256]{1,0:T(8,128)S(1)} %fusion.8), kind=kOutput, calls=%fused_computation.1 | convolution fusion | flops 1881276416 | bytes 14942208 | tf_op jit(solution)/shard_map/dot_general | solution.py:88
  224.3 86.2 %all_to_all.41 = bf16[16,16,7168]{2,1,0:T(8,128)(2,1)S(1)} all-to-all(bf16[16,16,7168]{2,1,0:T(8,128)(2,1)} %bitcast.59), channel_id=1, replica_groups=mesh['grp'=2,'tp'=16] {'tp'}, dimensions={0} | all-to-all | bytes 7340032 | tf_op jit(solution)/shard_map/all_to_all | solution.py:90
  310.5 2.0 copy.37
  312.6 1.7 fusion.2
  314.3 12.0 %reduce-scatter.5.cloned.1.call-done = bf16[8,7168]{1,0:T(8,128)(2,1)} async-done(((bf16[16,7168]{1,0:T(8,128)(2,1)}), bf16[8,7168]{1,0:T(8,128)(2,1)}) %reduce-scatter.5.cloned.1.call-update) | async-done | bytes 114704 | tf_op jit(solution)/shard_map/reduce_scatter | solution.py:99
  326.2 1.6 add_convert_fusion
  (28 shorter events, 0.9 us)
Async XLA Ops:
  6.5 1.3 copy-start
  6.5 109.3 %reduce-scatter.3.cloned.1.call-start = ((), (), s32[]{:S(2)}) async-start(), calls=%async_computation.5 | async-start | bytes 1949696 | tf_op jit(solution)/shard_map/reduce_scatter | solution.py:39
  13.8 37.3 %copy-start.1 = (bf16[1024,7168]{1,0:T(8,128)(2,1)S(1)}, bf16[1024,7168]{1,0:T(8,128)(2,1)}, u32[]{:S(2)}) copy-start(bf16[1024,7168]{1,0:T(8,128)(2,1)} %param.16) | copy-start | bytes 44040196
  17.7 32.9 %copy-start.3 = (bf16[8,512,128]{2,1,0:T(8,128)(2,1)S(1)}, bf16[8,512,128]{2,1,0:T(8,128)(2,1)}, u32[]{:S(2)}) copy-start(bf16[8,512,128]{2,1,0:T(8,128)(2,1)} %param.15) | copy-start | bytes 3145732
  51.1 3.8 %copy-start.6 = (s32[8,8]{1,0:T(8,128)S(1)}, s32[8,8]{1,0:T(8,128)}, u32[]{:S(2)}) copy-start(s32[8,8]{1,0:T(8,128)} %param.17) | copy-start | bytes 772
  51.1 3.9 %copy-start.7 = (bf16[8,8]{1,0:T(8,128)(2,1)S(1)}, bf16[8,8]{1,0:T(8,128)(2,1)}, u32[]{:S(2)}) copy-start(bf16[8,8]{1,0:T(8,128)(2,1)} %param.18) | copy-start | bytes 388
  51.1 64.7 %copy-start.4 = (bf16[8,7168]{1,0:T(8,128)(2,1)S(1)}, bf16[8,7168]{1,0:T(8,128)(2,1)}, u32[]{:S(2)}) copy-start(bf16[8,7168]{1,0:T(8,128)(2,1)} %param.14) | copy-start | bytes 344068
  54.8 271.4 %reduce-scatter.5.cloned.1.call-start = ((), (), s32[]{:S(2)}) async-start(), calls=%async_computation.6 | async-start | bytes 344064 | tf_op jit(solution)/shard_map/reduce_scatter | solution.py:99
  126.5 86.6 %copy-start.8 = (bf16[1,7168,256]{2,1,0:T(8,128)(2,1)S(1)}, bf16[1,7168,256]{2,1,0:T(8,128)(2,1)}, u32[]{:S(2)}) copy-start(bf16[1,7168,256]{2,1,0:T(8,128)(2,1)} %param.19) | copy-start | bytes 11010052
  211.3 1.8 copy-start.2
  312.5 13.7 %copy-start.5 = (bf16[8,7168]{1,0:T(8,128)(2,1)S(1)}, bf16[8,7168]{1,0:T(8,128)(2,1)}, u32[]{:S(2)}) copy-start(bf16[8,7168]{1,0:T(8,128)(2,1)} %reduce-scatter.3.cloned.1.call-done) | copy-start | bytes 344068
Sparse Core Ops, SparseCore 0:
  54.9 60.8 reduce-scatter.2
  314.4 11.8 reduce-scatter.4
where the time goes:
time: 335 us
  blocking collectives  213 us (64%)
  waiting for transfers between devices  67.7 us (20%)
  matrix products  28.2 us (8%)
  between operations  13.5 us (4%)
  local copies, waits for them, and re-layouts  7.06 us (2%)
  other arithmetic  4.83 us (1%)
    all_to_all x1, blocking collectives, body(): lax.all_to_all(partial_value.astype(jnp.bfloat16), 'tp', split_axis=0, co...  86.2 us
    all_to_all x1, blocking collectives, body(): lax.all_to_all(buffer, 'tp', split_axis=0, concat_axis=0, tiled=True)  84.8 us
    reduce_scatter x1, waiting for transfers between devices, body(): lax.psum_scatter(jnp.dot(values, out_weight, preferred_element_type=jnp.f...  55.7 us
    all_to_all x1, blocking collectives, body(): lax.all_to_all(context, 'tp', split_axis=1, concat_axis=0, tiled=True)  32.3 us
    reduce_scatter x1, waiting for transfers between devices, body(): lax.psum_scatter(terms.reshape(groups * rows_here, width).astype(jnp.bflo...  12 us
    dot_general x1, matrix products, body(): jnp.dot(hidden, w_down[0], preferred_element_type=jnp.float32)  10 us
  transfers between devices with their start and end apart: 2, of which 2 were waited for; matrix products, arithmetic and copies ran while one was open for 0% of the time, Pallas kernels for 0%

commit v1 on v0

v1 whole, which is shorter than its diff:
```python
import jax
import jax.numpy as jnp
from jax import lax
from jax.sharding import PartitionSpec as P


def body(
    queries,
    kv_cache,
    lengths,
    residual,
    uv_weight,
    out_weight,
    expert_ids,
    gate_values,
    w_gate,
    w_up,
    w_down,
):
    rows_here = residual.shape[0]
    latent = uv_weight.shape[1]
    width = residual.shape[1]
    span = kv_cache.shape[1]
    scores = jnp.einsum(
        "rhc,rlc->rhl", queries, kv_cache, preferred_element_type=jnp.float32
    ) * queries.shape[2] ** (-0.5)
    valid = lax.broadcasted_iota(jnp.int32, (1, 1, span), 2) < lengths[:, None, None]
    top = jnp.max(jnp.where(valid, scores, -jnp.inf), axis=-1, keepdims=True)
    expo = jnp.where(valid, jnp.exp(scores - top), 0.0)
    probs = (expo / jnp.sum(expo, axis=-1, keepdims=True)).astype(jnp.bfloat16)
    context = jnp.einsum(
        "rhl,rlc->rhc", probs, kv_cache[:, :, :latent], preferred_element_type=jnp.float32
    ).astype(jnp.bfloat16)
    grouped = lax.all_to_all(context, "tp", split_axis=1, concat_axis=0, tiled=True)
    values = jnp.einsum(
        "rhc,hcv->rhv", grouped, uv_weight, preferred_element_type=jnp.float32
    ).astype(jnp.bfloat16)
    values = values.reshape(values.shape[0], values.shape[1] * values.shape[2])
    attention = lax.psum_scatter(
        jnp.dot(values, out_weight, preferred_element_type=jnp.float32).astype(jnp.bfloat16),
        "tp",
        scatter_dimension=0,
        tiled=True,
    ).astype(jnp.float32)
    hidden_state = residual.astype(jnp.float32) + attention
    normed = (
        hidden_state
        * lax.rsqrt(jnp.mean(hidden_state * hidden_state, axis=-1, keepdims=True) + 1e-06)
    ).astype(jnp.bfloat16)
    experts = lax.axis_size("tp")
    me = lax.axis_index("tp")
    ids_hot = expert_ids[:, :, None] == lax.broadcasted_iota(jnp.int32, (1, 1, experts), 2)
    weights = jnp.sum(
        jnp.where(ids_hot, gate_values.astype(jnp.float32)[:, :, None], 0.0), axis=1
    ).astype(jnp.bfloat16)
    weights_all = lax.all_gather(weights, ("grp", "tp"), axis=0, tiled=True)
    own = lax.broadcasted_iota(jnp.int32, (1, experts), 1) == me
    weight = jnp.sum(
        jnp.where(own, weights_all.astype(jnp.float32), 0.0), axis=1, keepdims=True
    )
    rows_all = lax.all_gather(normed, ("grp", "tp"), axis=0, tiled=True)
    gate = jnp.dot(rows_all, w_gate[0], preferred_element_type=jnp.float32)
    up = jnp.dot(rows_all, w_up[0], preferred_element_type=jnp.float32)
    hidden = (jax.nn.silu(gate) * up * weight).astype(jnp.bfloat16)
    partial_value = jnp.dot(hidden, w_down[0], preferred_element_type=jnp.float32)
    routed = lax.psum_scatter(
        partial_value.astype(jnp.bfloat16), ("grp", "tp"), scatter_dimension=0, tiled=True
    ).astype(jnp.float32)
    return (hidden_state + routed).astype(jnp.bfloat16)


def solution(mesh):
    placed = (
        P(("grp", "tp"), None, None),
        P(("grp", "tp"), None, None),
        P(("grp", "tp")),
        P(("grp", "tp"), None),
        P("tp", None, None),
        P("tp", None),
        P(("grp", "tp"), None),
        P(("grp", "tp"), None),
        P("tp", None, "grp"),
        P("tp", None, "grp"),
        P("tp", "grp", None),
    )
    return jax.shard_map(
        body, mesh=mesh, in_specs=placed, out_specs=P(("grp", "tp"), None), check_vma=False
    )
```

time: 335 us -> 339 us (1.012)
  waiting for transfers between devices: 67.7 us -> 219 us
  blocking collectives: 213 us -> 72.1 us
  local copies, waits for them, and re-layouts: 7.06 us -> 1.08 us
    all_to_all x2 -> x0, blocking collectives: 171 us -> none  [the longest x1 86.2 us: body(): lax.all_to_all(partial_value.astype(jnp.bfloat16), 'tp', split_axis=0, co...]
    reduce_scatter x1, waiting for transfers between devices: 12 us -> 139 us  [body(): lax.psum_scatter(partial_value.astype(jnp.bfloat16), ('grp', 'tp'), scatt...]
    all_gather x2 -> x1, blocking collectives: 9.88 us -> 39.8 us  [body(): weights_all = lax.all_gather(weights, ('grp', 'tp'), axis=0, tiled=True)]
    all_gather x0 -> x1, waiting for transfers between devices: none -> 19.5 us  [body(): rows_all = lax.all_gather(normed, ('grp', 'tp'), axis=0, tiled=True)]
    reduce_scatter x1, waiting for transfers between devices: 55.7 us -> 60.9 us  [body(): lax.psum_scatter(jnp.dot(values, out_weight, preferred_element_type=jnp.f...]
    all_to_all x2 -> x0, local copies, waits for them, and re-layouts: 4.02 us -> none  [the longest x1 2.01 us: body(): lax.all_to_all(buffer, 'tp', split_axis=0, concat_axis=0, tiled=True)]
  transfers between devices with their start and end apart: 2 -> 3, of which waited for: 2 -> 3; matrix products, arithmetic and copies ran while one was open for 0% -> 0% of each run, Pallas kernels for 0% -> 0%
where the time goes in v1:
time: 339 us
  waiting for transfers between devices  219 us (65%)
  blocking collectives  72.1 us (21%)
  matrix products  28.2 us (8%)
  between operations  13.2 us (4%)
  other arithmetic  5.35 us (2%)
    reduce_scatter x1, waiting for transfers between devices, body(): lax.psum_scatter(partial_value.astype(jnp.bfloat16), ('grp', 'tp'), scatt...  139 us
    reduce_scatter x1, waiting for transfers between devices, body(): lax.psum_scatter(jnp.dot(values, out_weight, preferred_element_type=jnp.f...  60.9 us
    all_gather x1, blocking collectives, body(): weights_all = lax.all_gather(weights, ('grp', 'tp'), axis=0, tiled=True)  39.8 us
    all_to_all x1, blocking collectives, body(): lax.all_to_all(context, 'tp', split_axis=1, concat_axis=0, tiled=True)  32.3 us
    all_gather x1, waiting for transfers between devices, body(): rows_all = lax.all_gather(normed, ('grp', 'tp'), axis=0, tiled=True)  19.5 us
    dot_general x1, matrix products, body(): jnp.dot(hidden, w_down[0], preferred_element_type=jnp.float32)  10 us
  transfers between devices with their start and end apart: 3, of which 3 were waited for; matrix products, arithmetic and copies ran while one was open for 0% of the time, Pallas kernels for 0%

profile of v1, /device:TPU:0, one launch (start us, length us, event | category | flops | bytes accessed | tf_op | source)
XLA Modules:
  0.0 339.3 jit_solution(9301435739976019247)
XLA Ops:
  6.5 0.8 iota_compare_fusion.1
  7.4 0.5 copy-done
  7.8 6.0 %fusion.42 = (f32[8,128]{1,0:T(8,128)S(1)}, f32[8,128,512]{2,1,0:T(8,128)S(1)}) fusion(pred[8,512]{1,0:T(8,128)(4,1)S(1)} %iota_compare_fusion.1, bf16[8,128,576]{1,2,0:T(8,128)(2,1)S(1)} %copy-done, bf16[8,512,576]{1,2,0:T(8,128)(2,1)} %param.12), kind=kOutput, calls=%fused_computation.46 | convolution fusion | flops 1211105792 | bytes 8003584 | tf_op jit(solution)/shard_map/sub | solution.py:29
  13.8 3.8 %fusion.12 = bf16[8,128,512]{2,1,0:T(8,128)(2,1)S(1)} fusion(bf16[8,512,576]{1,2,0:T(8,128)(2,1)} %param.12, f32[8,128,512]{2,1,0:T(8,128)S(1)} %get-tuple-element.6, f32[8,128]{1,0:T(8,128)S(1)} %get-tuple-element.5), kind=kOutput, calls=%fused_computation.15 | convolution fusion | flops 538443776 | bytes 7344128 | tf_op jit(solution)/shard_map/rhl,rlc->rhc/dot_general | solution.py:31
  17.7 0.6 copy.20
  18.3 32.3 %all_to_all.18 = bf16[8,128,512]{2,0,1:T(8,128)(2,1)S(1)} all-to-all(bf16[8,128,512]{2,0,1:T(8,128)(2,1)S(1)} %copy.20), channel_id=1, replica_groups=mesh['grp'=2,'tp'=16] {'tp'}, dimensions={1} | all-to-all | bytes 2097152 | tf_op jit(solution)/shard_map/all_to_all | solution.py:34
  50.5 0.5 convolution_convert_fusion.2
  51.1 3.7 %convolution_convert_fusion.1 = bf16[128,7168]{1,0:T(8,128)(2,1)} fusion(bf16[128,1024]{0,1:T(8,128)(2,1)S(1)} %bitcast.36, bf16[1024,7168]{1,0:T(8,128)(2,1)S(1)} %copy-done.1), kind=kOutput, calls=%fused_computation.2 | convolution fusion | flops 1879965696 | bytes 16777216 | tf_op jit(solution)/shard_map/dot_general | solution.py:40
  54.8 0.0 reduce-scatter.3.cloned.1.call-update
  54.8 0.0 all-gather.2.cloned.1.call-start
  54.8 60.9 %reduce-scatter.3.cloned.1.call-done = bf16[8,7168]{1,0:T(8,128)(2,1)} async-done(((bf16[128,7168]{1,0:T(8,128)(2,1)}), bf16[8,7168]{1,0:T(8,128)(2,1)}) %reduce-scatter.3.cloned.1.call-update) | async-done | bytes 114704 | tf_op jit(solution)/shard_map/reduce_scatter | solution.py:39
  115.7 1.1 multiply_reduce_fusion
  116.8 1.6 multiply_convert_fusion
  118.5 0.0 all-gather.2.cloned.1.call-update
  118.5 0.0 reduce-scatter.5.cloned.1.call-start
  118.6 0.1 select_reduce_fusion.2
  118.7 39.8 %all_gather.7 = bf16[256,16]{1,0:T(8,128)(2,1)S(1)} all-gather(bf16[8,16]{1,0:T(8,128)(2,1)S(1)} %select_reduce_fusion.2), channel_id=1, replica_groups=mesh['grp'=2,'tp'=16] {'grp','tp'}, dimensions={0}, use_global_device_ids=true | all-gather | bytes 8448 | tf_op jit(solution)/shard_map/all_gather | solution.py:56
  158.5 0.1 select_reduce_fusion.1
  158.6 19.5 %all-gather.2.cloned.1.call-done = bf16[256,7168]{1,0:T(8,128)(2,1)} async-done(((bf16[8,7168]{1,0:T(8,128)(2,1)}), bf16[256,7168]{1,0:T(8,128)(2,1)}) %all-gather.2.cloned.1.call-update) | async-done | bytes 3670032 | tf_op jit(solution)/shard_map/all_gather | solution.py:61
  178.2 4.3 %fusion.6 = f32[256,256]{1,0:T(8,128)S(1)} fusion(bf16[256,7168]{1,0:T(8,128)(2,1)} %all-gather.2.cloned.1.call-done, bf16[1,7168,256]{2,1,0:T(8,128)(2,1)} %param.19), kind=kOutput, calls=%fused_computation.8 | convolution fusion | flops 939524096 | bytes 7602176 | tf_op jit(solution)/shard_map/dot_general | solution.py:62
  182.4 10.0 %convolution_convert_fusion = bf16[256,7168]{1,0:T(8,128)(2,1)} fusion(bf16[1,256,7168]{2,1,0:T(8,128)(2,1)} %param.21, bf16[256,7168]{1,0:T(8,128)(2,1)} %all-gather.2.cloned.1.call-done, bf16[1,7168,256]{2,1,0:T(8,128)(2,1)} %param.20, f32[256,256]{1,0:T(8,128)S(1)} %fusion.6, f32[256]{0:T(256)S(1)} %select_reduce_fusion.1), kind=kOutput, calls=%fused_computation.1 | convolution fusion | flops 1881341952 | bytes 14943232 | tf_op jit(solution)/shard_map/dot_general | solution.py:65
  192.4 0.0 reduce-scatter.5.cloned.1.call-update
  192.5 138.7 %reduce-scatter.5.cloned.1.call-done = bf16[8,7168]{1,0:T(8,128)(2,1)} async-done(((bf16[256,7168]{1,0:T(8,128)(2,1)}), bf16[8,7168]{1,0:T(8,128)(2,1)}) %reduce-scatter.5.cloned.1.call-update) | async-done | bytes 114704 | tf_op jit(solution)/shard_map/reduce_scatter | solution.py:66
  331.2 1.6 add_convert_fusion
  (17 shorter events, 0.1 us)
Async XLA Ops:
  6.5 1.3 copy-start
  6.5 109.2 %reduce-scatter.3.cloned.1.call-start = ((), (), s32[]{:S(2)}) async-start(), calls=%async_computation.3 | async-start | bytes 1949696 | tf_op jit(solution)/shard_map/reduce_scatter | solution.py:39
  13.8 37.3 %copy-start.1 = (bf16[1024,7168]{1,0:T(8,128)(2,1)S(1)}, bf16[1024,7168]{1,0:T(8,128)(2,1)}, u32[]{:S(2)}) copy-start(bf16[1024,7168]{1,0:T(8,128)(2,1)} %param.16) | copy-start | bytes 44040196
  17.7 32.9 %copy-start.2 = (bf16[8,512,128]{2,1,0:T(8,128)(2,1)S(1)}, bf16[8,512,128]{2,1,0:T(8,128)(2,1)}, u32[]{:S(2)}) copy-start(bf16[8,512,128]{2,1,0:T(8,128)(2,1)} %param.15) | copy-start | bytes 3145732
  51.1 64.7 %copy-start.3 = (bf16[8,7168]{1,0:T(8,128)(2,1)S(1)}, bf16[8,7168]{1,0:T(8,128)(2,1)}, u32[]{:S(2)}) copy-start(bf16[8,7168]{1,0:T(8,128)(2,1)} %param.14) | copy-start | bytes 344068
  51.1 67.5 %copy-start.6 = (bf16[8,8]{1,0:T(8,128)(2,1)S(1)}, bf16[8,8]{1,0:T(8,128)(2,1)}, u32[]{:S(2)}) copy-start(bf16[8,8]{1,0:T(8,128)(2,1)} %param.18) | copy-start | bytes 388
  51.1 67.5 %copy-start.5 = (s32[8,8]{1,0:T(8,128)S(1)}, s32[8,8]{1,0:T(8,128)}, u32[]{:S(2)}) copy-start(s32[8,8]{1,0:T(8,128)} %param.17) | copy-start | bytes 772
  54.8 123.4 %all-gather.2.cloned.1.call-start = ((), (), s32[]{:S(2)}) async-start(), calls=%async_computation.4 | async-start | bytes 3784704 | tf_op jit(solution)/shard_map/all_gather | solution.py:61
  118.5 212.7 %reduce-scatter.5.cloned.1.call-start = ((), (), s32[]{:S(2)}) async-start(), calls=%async_computation.5 | async-start | bytes 3784704 | tf_op jit(solution)/shard_map/reduce_scatter | solution.py:66
  192.4 138.7 %copy-start.4 = (bf16[8,7168]{1,0:T(8,128)(2,1)S(1)}, bf16[8,7168]{1,0:T(8,128)(2,1)}, u32[]{:S(2)}) copy-start(bf16[8,7168]{1,0:T(8,128)(2,1)} %reduce-scatter.3.cloned.1.call-done) | copy-start | bytes 344068
Sparse Core Ops, SparseCore 0:
  54.9 60.7 reduce-scatter.2
  118.6 59.5 all-gather.1
  192.6 138.5 reduce-scatter.4

commit v2 on v1

--- a/solution.py
+++ b/solution.py
@@ -1,7 +1,250 @@
+import functools
 import jax
 import jax.numpy as jnp
 from jax import lax
+from jax.experimental import pallas as pl
+from jax.experimental.pallas import tpu as pltpu
 from jax.sharding import PartitionSpec as P
+
+MESH = pl.DeviceIdType.MESH
+F32, BF16 = jnp.float32, jnp.bfloat16
+
+
+def axis_bits(groups, peers):
+    grp = [("grp", 1, False)] if groups == 2 else [("grp", 2, True), ("grp", 1, False)]
+    tp = [("tp", peers // 2, True), ("tp", peers // 4, False)]
+    tp += [("tp", 2, False)] if peers // 8 == 2 else [("tp", 4, True), ("tp", 2, False)]
+    return grp, tp
+
+
+def chain_orders(bits):
+    near = [i for i, b in enumerate(bits) if not b[2]]
+    far = [i for i, b in enumerate(bits) if b[2]]
+    turn = lambda xs, k: xs[k % len(xs):] + xs[: k % len(xs)] if xs else []
+    return [turn(near, k) + turn(far, k) for k in range(len(near))]
+
+
+def column_parts(half, n):
+    tiles = half // 128
+    cuts = [128 * (tiles * k // n) for k in range(n + 1)]
+    return [(cuts[k], cuts[k + 1] - cuts[k]) for k in range(n)]
+
+
+class Place:
+    def __init__(self, bits):
+        self.g, self.t = lax.axis_index("grp"), lax.axis_index("tp")
+        self.core = self.t % 2
+        self.sibling = (self.g, self.t + 1 - 2 * self.core)
+        self.mine, self.partner = [], []
+        for axis, value, _ in bits:
+            at = self.g if axis == "grp" else self.t
+            bit = (at // value) % 2
+            moved = at + value * (1 - 2 * bit)
+            self.mine.append(bit)
+            self.partner.append((moved, self.t) if axis == "grp" else (self.g, moved))
+
+    def greet(self):
+        barrier = pltpu.get_barrier_semaphore()
+        others = [self.sibling] + self.partner
+        for other in others:
+            pl.semaphore_signal(barrier, inc=1, device_id=other, device_id_type=MESH)
+        pl.semaphore_wait(barrier, len(others))
+
+
+def send(src, dst, sems, at, to):
+    copy = pltpu.make_async_remote_copy(
+        src_ref=src,
+        dst_ref=dst,
+        send_sem=sems[0].at[at],
+        recv_sem=sems[1].at[at],
+        device_id=to,
+        device_id_type=MESH,
+    )
+    copy.start()
+    return copy
+
+
+def columns(start, size):
+    return pl.ds(pl.multiple_of(start, 128), size)
+
+
+def scatter_scratch(bits, half):
+    shapes = [pltpu.VMEM((2,) * len(bits) + (16, half), BF16), pltpu.VMEM((2, 8, half), F32)]
+    shapes += [pltpu.VMEM((8, half), F32)]
+    orders = chain_orders(bits)
+    for _, width in column_parts(half, len(orders)):
+        for done in range(len(bits) + 1):
+            shapes.append(pltpu.VMEM((2,) * (len(bits) - done) + (16, width), BF16))
+    count = len(orders) * (len(bits) + 2)
+    return shapes + [pltpu.SemaphoreType.DMA((count,)), pltpu.SemaphoreType.DMA((count,))]
+
+
+def reduce_scatter(bits, place, half, x_ref, out_ref, scratch):
+    held, own, swapped = scratch[:3]
+    sems = scratch[-2:]
+    orders = chain_orders(bits)
+    parts = column_parts(half, len(orders))
+    n = len(bits)
+    landed = [scratch[3 + k * (n + 1): 3 + (k + 1) * (n + 1)] for k in range(len(orders))]
+    every = (slice(None),) * (n + 1)
+    core = place.core
+    copies, now = [], []
+
+    def launch(*what):
+        copy = send(*what)
+        copies.append(copy)
+        return copy
+
+    for k, (start, width) in enumerate(parts):
+        src = x_ref.at[every + (columns((1 - core) * half + start, width),)]
+        now.append(launch(src, landed[k][0], sems, k * (n + 2), place.sibling))
+    for stage in range(n + 1):
+        for k, (start, width) in enumerate(parts):
+            here = pl.ds(start, width)
+            now[k].wait_recv()
+            done = orders[k][:stage]
+            keep = tuple(place.mine[i] if i in done else slice(None) for i in range(n)) + (slice(None),)
+            base = (
+                x_ref[every + (columns(core * half + start, width),)]
+                if stage == 0
+                else held[keep + (here,)]
+            )
+            total = base.astype(F32) + landed[k][stage][...].astype(F32)
+            if stage < n:
+                held[keep + (here,)] = total.astype(BF16)
+                bit = orders[k][stage]
+                away = tuple(
+                    1 - place.mine[i] if i == bit else keep[i] for i in range(n)
+                ) + (slice(None), here)
+                now[k] = launch(
+                    held.at[away], landed[k][stage + 1], sems, k * (n + 2) + stage + 1, place.partner[bit]
+                )
+            else:
+                own[0, :, here] = total[:8]
+                own[1, :, here] = total[8:]
+                now[k] = launch(
+                    own.at[1 - core, :, here], swapped.at[:, here], sems, k * (n + 2) + n + 1, place.sibling
+                )
+    for k, (start, width) in enumerate(parts):
+        here = pl.ds(start, width)
+        out_ref[:, columns(core * half + start, width)] = own[core, :, here]
+        now[k].wait_recv()
+        out_ref[:, columns((1 - core) * half + start, width)] = swapped[:, here]
+    for copy in copies:
+        copy.wait_send()
+
+
+def gather_scratch(bits, half):
+    orders = chain_orders(bits)
+    count = len(orders) * (len(bits) + 2)
+    return [
+        pltpu.VMEM((8, half), F32),
+        pltpu.SemaphoreType.DMA((count,)),
+        pltpu.SemaphoreType.DMA((count,)),
+    ]
+
+
+def gather(bits, place, half, rows_ref, out_ref, scratch):
+    swapped, sems = scratch[0], scratch[1:]
+    orders = chain_orders(bits)
+    parts = column_parts(half, len(orders))
+    n = len(bits)
+    core = place.core
+    copies, now = [], []
+
+    def launch(*what):
+        copy = send(*what)
+        copies.append(copy)
+        return copy
+
+    for k, (start, width) in enumerate(parts):
+        src = rows_ref.at[:, columns((1 - core) * half + start, width)]
+        now.append(launch(src, swapped.at[:, pl.ds(start, width)], sems, k * (n + 2), place.sibling))
+    for stage in range(n + 1):
+        for k, (start, width) in enumerate(parts):
+            here = columns(core * half + start, width)
+            now[k].wait_recv()
+            order = orders[k][::-1]
+            if stage == 0:
+                mine, other = rows_ref[:, here], swapped[:, pl.ds(start, width)]
+                first = jnp.where(core == 0, mine, other)
+                second = jnp.where(core == 0, other, mine)
+                block = jnp.concatenate([first, second], axis=0).astype(BF16)
+                out_ref[tuple(place.mine) + (slice(None), here)] = block
+            done = order[:stage]
+            at = tuple(slice(None) if i in done else place.mine[i] for i in range(n))
+            part = out_ref.at[at + (slice(None), here)]
+            to = place.partner[order[stage]] if stage < n else place.sibling
+            now[k] = launch(part, part, sems, k * (n + 2) + stage + 1, to)
+    for k in range(len(parts)):
+        now[k].wait_recv()
+    for copy in copies:
+        copy.wait_send()
+
+
+def middle_kernel(tp_bits, all_bits, x_ref, residual_ref, hidden_ref, rows_ref, normed, *scratch):
+    half = residual_ref.shape[1] // 2
+    place_all = Place(all_bits)
+    place = Place(tp_bits)
+    place_all.greet()
+    cut = len(scatter_scratch(tp_bits, half))
+    reduce_scatter(tp_bits, place, half, x_ref, hidden_ref, scratch[:cut])
+    state = hidden_ref[...] + residual_ref[...].astype(F32)
+    hidden_ref[...] = state
+    normed[...] = state * lax.rsqrt(jnp.mean(state * state, axis=-1, keepdims=True) + 1e-06)
+    gather(all_bits, place_all, half, normed, rows_ref, scratch[cut:])
+
+
+def final_kernel(all_bits, x_ref, hidden_ref, out_ref, routed, *scratch):
+    half = hidden_ref.shape[1] // 2
+    place = Place(all_bits)
+    place.greet()
+    reduce_scatter(all_bits, place, half, x_ref, routed, scratch)
+    out_ref[...] = (routed[...] + hidden_ref[...]).astype(out_ref.dtype)
+
+
+VMEM = pl.BlockSpec(memory_space=pltpu.VMEM)
+
+
+def middle(part, residual, groups, peers):
+    width = residual.shape[1]
+    grp_bits, tp_bits = axis_bits(groups, peers)
+    both = grp_bits + tp_bits
+    rows = groups * peers * 8
+    need = width * 2 * (3 * part.shape[0] + rows) + (12 << 20)
+    hidden, gathered = pl.pallas_call(
+        functools.partial(middle_kernel, tp_bits, both),
+        out_shape=(
+            jax.ShapeDtypeStruct((8, width), F32),
+            jax.ShapeDtypeStruct((2,) * len(both) + (16, width), BF16),
+        ),
+        in_specs=[VMEM, VMEM],
+        out_specs=(VMEM, VMEM),
+        scratch_shapes=[pltpu.VMEM((8, width), F32)]
+        + scatter_scratch(tp_bits, width // 2)
+        + gather_scratch(both, width // 2),
+        compiler_params=pltpu.CompilerParams(
+            collective_id=0, has_side_effects=True, vmem_limit_bytes=need
+        ),
+    )(part.reshape((2,) * len(tp_bits) + (16, width)), residual)
+    return hidden, gathered.reshape(rows, width)
+
+
+def final(part, hidden, groups, peers):
+    width = hidden.shape[1]
+    grp_bits, tp_bits = axis_bits(groups, peers)
+    both = grp_bits + tp_bits
+    need = width * 2 * 3 * part.shape[0] + (12 << 20)
+    return pl.pallas_call(
+        functools.partial(final_kernel, both),
+        out_shape=jax.ShapeDtypeStruct((8, width), BF16),
+        in_specs=[VMEM, VMEM],
+        out_specs=VMEM,
+        scratch_shapes=[pltpu.VMEM((8, width), F32)] + scatter_scratch(both, width // 2),
+        compiler_params=pltpu.CompilerParams(
+            collective_id=1, has_side_effects=True, vmem_limit_bytes=need
+        ),
+    )(part.reshape((2,) * len(both) + (16, width)), hidden)
 
 
 def body(
@@ -36,17 +279,9 @@
         "rhc,hcv->rhv", grouped, uv_weight, preferred_element_type=jnp.float32
     ).astype(jnp.bfloat16)
     values = values.reshape(values.shape[0], values.shape[1] * values.shape[2])
-    attention = lax.psum_scatter(
-        jnp.dot(values, out_weight, preferred_element_type=jnp.float32).astype(jnp.bfloat16),
-        "tp",
-        scatter_dimension=0,
-        tiled=True,
-    ).astype(jnp.float32)
-    hidden_state = residual.astype(jnp.float32) + attention
-    normed = (
-        hidden_state
-        * lax.rsqrt(jnp.mean(hidden_state * hidden_state, axis=-1, keepdims=True) + 1e-06)
-    ).astype(jnp.bfloat16)
+    groups, peers = lax.axis_size("grp"), lax.axis_size("tp")
+    attention = jnp.dot(values, out_weight, preferred_element_type=jnp.float32).astype(BF16)
+    hidden_state, rows_all = middle(attention, residual, groups, peers)
     experts = lax.axis_size("tp")
     me = lax.axis_index("tp")
     ids_hot = expert_ids[:, :, None] == lax.broadcasted_iota(jnp.int32, (1, 1, experts), 2)
@@ -58,15 +293,11 @@
     weight = jnp.sum(
         jnp.where(own, weights_all.astype(jnp.float32), 0.0), axis=1, keepdims=True
     )
-    rows_all = lax.all_gather(normed, ("grp", "tp"), axis=0, tiled=True)
     gate = jnp.dot(rows_all, w_gate[0], preferred_element_type=jnp.float32)
     up = jnp.dot(rows_all, w_up[0], preferred_element_type=jnp.float32)
     hidden = (jax.nn.silu(gate) * up * weight).astype(jnp.bfloat16)
     partial_value = jnp.dot(hidden, w_down[0], preferred_element_type=jnp.float32)
-    routed = lax.psum_scatter(
-        partial_value.astype(jnp.bfloat16), ("grp", "tp"), scatter_dimension=0, tiled=True
-    ).astype(jnp.float32)
-    return (hidden_state + routed).astype(jnp.bfloat16)
+    return final(partial_value.astype(jnp.bfloat16), hidden_state, groups, peers)
 
 
 def solution(mesh):

time: 339 us -> 172 us (0.51)
  waiting for transfers between devices: 219 us -> 0.01 us
  Pallas kernels: 0 us -> 75 us
  blocking collectives: 72.1 us -> 52.9 us
  between operations: 13.2 us -> 0.16 us
  starting transfers between devices: 0.09 us -> 7.39 us
  local copies, waits for them, and re-layouts: 1.08 us -> 6.53 us
  other arithmetic: 5.35 us -> 1.04 us
    reduce_scatter x2 -> x0, waiting for transfers between devices: 200 us -> none  [the longest x1 139 us: body(): lax.psum_scatter(partial_value.astype(jnp.bfloat16), ('grp', 'tp'), scatt...]
    pallas_call x0 -> x2, Pallas kernels: none -> 75 us  [the longest x1 47.2 us: middle(): pl.pallas_call(functools.partial(middle_kernel, tp_bits, both), out_shape...]
    all_to_all x1 -> x0, blocking collectives: 32.3 us -> none  [body(): lax.all_to_all(context, 'tp', split_axis=1, concat_axis=0, tiled=True)]
    all_gather x1 -> x0, waiting for transfers between devices: 19.5 us -> none  [body(): rows_all = lax.all_gather(normed, ('grp', 'tp'), axis=0, tiled=True)]
    all_gather x1, blocking collectives: 39.8 us -> 52.9 us  [body(): weights_all = lax.all_gather(weights, ('grp', 'tp'), axis=0, tiled=True)]
    all_to_all x0 -> x1, starting transfers between devices: none -> 7.39 us  [body(): lax.all_to_all(context, 'tp', split_axis=1, concat_axis=0, tiled=True)]
    unnamed x14 -> x17, local copies, waits for them, and re-layouts: 0.5 us -> 4.96 us
    dot_general x1, matrix products: 3.66 us -> 7.49 us  [body(): jnp.dot(values, out_weight, preferred_element_type=jnp.float32).astype(BF16)]
  transfers between devices with their start and end apart: 3 -> 1, of which waited for: 3 -> 0; matrix products, arithmetic and copies ran while one was open for 0% -> 0% of each run, Pallas kernels for 0% -> 0%
where the time goes in v2:
time: 172 us
  Pallas kernels  75 us (44%)
  blocking collectives  52.9 us (31%)
  matrix products  28.9 us (17%)
  starting transfers between devices  7.39 us (4%)
  local copies, waits for them, and re-layouts  6.53 us (4%)
    all_gather x1, blocking collectives, body(): weights_all = lax.all_gather(weights, ('grp', 'tp'), axis=0, tiled=True)  52.9 us
    pallas_call x1, Pallas kernels, middle(): pl.pallas_call(functools.partial(middle_kernel, tp_bits, both), out_shape...  47.2 us
    pallas_call x1, Pallas kernels, final(): pl.pallas_call(functools.partial(final_kernel, both), out_shape=jax.Shape...  27.8 us
    dot_general x1, matrix products, body(): jnp.dot(hidden, w_down[0], preferred_element_type=jnp.float32)  10 us
    dot_general x1, matrix products, body(): jnp.dot(values, out_weight, preferred_element_type=jnp.float32).astype(BF16)  7.49 us
    all_to_all x1, starting transfers between devices, body(): lax.all_to_all(context, 'tp', split_axis=1, concat_axis=0, tiled=True)  7.39 us
    sub x1, matrix products, body(): expo = jnp.where(valid, jnp.exp(scores - top), 0.0)  5.96 us
    unnamed x17, local copies, waits for them, and re-layouts  4.96 us
  transfers between devices with their start and end apart: 1, of which 0 were waited for; matrix products, arithmetic and copies ran while one was open for 0% of the time, Pallas kernels for 0%

profile of v2, /device:TPU:0, one launch (start us, length us, event | category | flops | bytes accessed | tf_op | source)
XLA Modules:
  0.0 171.9 jit_solution(1323090630942179537)
XLA Ops:
  0.0 0.8 iota_compare_fusion.1
  0.8 0.5 copy-done
  1.3 6.0 %fusion.42 = (f32[8,128]{1,0:T(8,128)S(1)}, f32[8,128,512]{2,1,0:T(8,128)S(1)}) fusion(pred[8,512]{1,0:T(8,128)(4,1)S(1)} %iota_compare_fusion.1, bf16[8,128,576]{1,2,0:T(8,128)(2,1)S(1)} %copy-done, bf16[8,512,576]{1,2,0:T(8,128)(2,1)} %param.12), kind=kOutput, calls=%fused_computation.41 | convolution fusion | flops 1211105792 | bytes 8003584 | tf_op jit(solution)/shard_map/sub | solution.py:272
  7.3 3.7 %fusion.12 = bf16[8,128,512]{2,1,0:T(8,128)(2,1)S(1)} fusion(bf16[8,512,576]{1,2,0:T(8,128)(2,1)} %param.12, f32[8,128,512]{2,1,0:T(8,128)S(1)} %get-tuple-element.10, f32[8,128]{1,0:T(8,128)S(1)} %get-tuple-element.9), kind=kOutput, calls=%fused_computation.15 | convolution fusion | flops 538443776 | bytes 7344128 | tf_op jit(solution)/shard_map/rhl,rlc->rhc/dot_general | solution.py:274
  11.0 0.0 copy-start.6
  11.0 0.0 copy-start.5
  11.0 0.0 copy-start.4
  11.0 1.6 copy.20
  12.6 7.4 %all-to-all-start = ((bf16[8,128,512]{2,0,1:T(8,128)(2,1)}), bf16[8,128,512]{2,0,1:T(8,128)(2,1)S(1)}, u32[]{:S(2)}, u32[]{:S(2)}) async-start(bf16[8,128,512]{2,0,1:T(8,128)(2,1)} %copy.20), calls=%async_computation | async-start | bytes 2097152 | tf_op jit(solution)/shard_map/all_to_all | solution.py:277
  20.0 0.1 select_reduce_fusion.2
  20.1 52.9 %all_gather.3 = bf16[256,16]{1,0:T(8,128)(2,1)S(1)} all-gather(bf16[8,16]{1,0:T(8,128)(2,1)S(1)} %select_reduce_fusion.2), channel_id=1, replica_groups=mesh['grp'=2,'tp'=16] {'grp','tp'}, dimensions={0}, use_global_device_ids=true | all-gather | bytes 8448 | tf_op jit(solution)/shard_map/all_gather | solution.py:291
  73.1 0.1 select_reduce_fusion.1
  73.2 0.0 all-to-all-done
  73.2 0.5 convolution_convert_fusion.2
  73.7 0.0 copy-start.3
  73.7 0.0 copy-start.7
  73.7 7.5 %convolution_convert_fusion.1 = bf16[128,7168]{1,0:T(8,128)(2,1)S(1)} fusion(bf16[128,1024]{0,1:T(8,128)(2,1)S(1)} %bitcast.43, bf16[1024,7168]{1,0:T(8,128)(2,1)} %param.16), kind=kOutput, calls=%fused_computation.2 | convolution fusion | flops 1879965696 | bytes 16777216 | tf_op jit(solution)/shard_map/dot_general | solution.py:283
  81.3 47.2 %shard_map.109 = (f32[8,7168]{1,0:T(8,128)S(1)}, bf16[2,2,2,2,16,7168]{5,4,3,2,1,0:T(8,128)(2,1)S(1)}) custom-call(bf16[2,2,2,16,7168]{4,3,2,1,0:T(8,128)(2,1)S(1)} %bitcast.39, bf16[8,7168]{1,0:T(8,128)(2,1)S(1)} %copy-done.3), custom_call_target="tpu_custom_call" | custom-call | tf_op jit(solution)/shard_map/pallas_call | solution.py:215
  128.4 1.8 %copy-done.2 = bf16[2,2,2,2,16,7168]{5,4,3,2,1,0:T(8,128)(2,1)} copy-done((bf16[2,2,2,2,16,7168]{5,4,3,2,1,0:T(8,128)(2,1)}, bf16[2,2,2,2,16,7168]{5,4,3,2,1,0:T(8,128)(2,1)S(1)}, u32[]{:S(2)}) %copy-start.2) | copy-done | bytes 3670040
  130.2 1.2 fusion.6
  131.4 10.0 %convolution_convert_fusion = bf16[256,7168]{1,0:T(8,128)(2,1)} fusion(bf16[1,256,7168]{2,1,0:T(8,128)(2,1)} %param.21, bf16[256,7168]{1,0:T(8,128)(2,1)} %bitcast.41, bf16[1,7168,256]{2,1,0:T(8,128)(2,1)} %param.20, f32[256,256]{1,0:T(8,128)S(1)} %fusion.6, f32[256]{0:T(256)S(1)} %select_reduce_fusion.1), kind=kOutput, calls=%fused_computation.1 | convolution fusion | flops 1881341952 | bytes 14943232 | tf_op jit(solution)/shard_map/dot_general | solution.py:299
  141.4 2.0 %copy-done.1 = bf16[256,7168]{1,0:T(8,128)(2,1)S(1)} copy-done((bf16[256,7168]{1,0:T(8,128)(2,1)S(1)}, bf16[256,7168]{1,0:T(8,128)(2,1)}, u32[]{:S(2)}) %copy-start.1) | copy-done | bytes 3670040
  143.5 27.8 %shard_map.110 = bf16[8,7168]{1,0:T(8,128)(2,1)S(1)} custom-call(bf16[2,2,2,2,16,7168]{5,4,3,2,1,0:T(8,128)(2,1)S(1)} %bitcast.38, f32[8,7168]{1,0:T(8,128)S(1)} %get-tuple-element.8.hidden_ref), custom_call_target="tpu_custom_call" | custom-call | tf_op jit(solution)/shard_map/pallas_call | solution.py:238
  171.3 0.6 copy.32
  (10 shorter events, 0.0 us)
Async XLA Ops:
  0.0 1.3 copy-start
  11.0 9.0 %copy-start.6 = (bf16[8,8]{1,0:T(8,128)(2,1)S(1)}, bf16[8,8]{1,0:T(8,128)(2,1)}, u32[]{:S(2)}) copy-start(bf16[8,8]{1,0:T(8,128)(2,1)} %param.18) | copy-start | bytes 388
  11.0 9.0 %copy-start.5 = (s32[8,8]{1,0:T(8,128)S(1)}, s32[8,8]{1,0:T(8,128)}, u32[]{:S(2)}) copy-start(s32[8,8]{1,0:T(8,128)} %param.17) | copy-start | bytes 772
  11.0 62.2 %copy-start.4 = (bf16[8,512,128]{2,1,0:T(8,128)(2,1)S(1)}, bf16[8,512,128]{2,1,0:T(8,128)(2,1)}, u32[]{:S(2)}) copy-start(bf16[8,512,128]{2,1,0:T(8,128)(2,1)} %param.15) | copy-start | bytes 3145732
  12.6 60.6 %all-to-all-start = ((bf16[8,128,512]{2,0,1:T(8,128)(2,1)}), bf16[8,128,512]{2,0,1:T(8,128)(2,1)S(1)}, u32[]{:S(2)}, u32[]{:S(2)}) async-start(bf16[8,128,512]{2,0,1:T(8,128)(2,1)} %copy.20), calls=%async_computation | async-start | bytes 2097152 | tf_op jit(solution)/shard_map/all_to_all | solution.py:277
  73.7 7.5 %copy-start.3 = (bf16[8,7168]{1,0:T(8,128)(2,1)S(1)}, bf16[8,7168]{1,0:T(8,128)(2,1)}, u32[]{:S(2)}) copy-start(bf16[8,7168]{1,0:T(8,128)(2,1)} %residual_ref.1) | copy-start | bytes 344068
  73.7 56.5 %copy-start.7 = (bf16[1,7168,256]{2,1,0:T(8,128)(2,1)S(1)}, bf16[1,7168,256]{2,1,0:T(8,128)(2,1)}, u32[]{:S(2)}) copy-start(bf16[1,7168,256]{2,1,0:T(8,128)(2,1)} %param.19) | copy-start | bytes 11010052
  128.4 1.8 %copy-start.2 = (bf16[2,2,2,2,16,7168]{5,4,3,2,1,0:T(8,128)(2,1)}, bf16[2,2,2,2,16,7168]{5,4,3,2,1,0:T(8,128)(2,1)S(1)}, u32[]{:S(2)}) copy-start(bf16[2,2,2,2,16,7168]{5,4,3,2,1,0:T(8,128)(2,1)S(1)} %get-tuple-element.7) | copy-start | bytes 11010052
  141.4 2.0 %copy-start.1 = (bf16[256,7168]{1,0:T(8,128)(2,1)S(1)}, bf16[256,7168]{1,0:T(8,128)(2,1)}, u32[]{:S(2)}) copy-start(bf16[256,7168]{1,0:T(8,128)(2,1)} %convolution_convert_fusion) | copy-start | bytes 11010052

commit v3 on v2

--- a/solution.py
+++ b/solution.py
@@ -6,6 +6,7 @@
 from jax.experimental.pallas import tpu as pltpu
 from jax.sharding import PartitionSpec as P
 
+TILE = 256
 MESH = pl.DeviceIdType.MESH
 F32, BF16 = jnp.float32, jnp.bfloat16
 
@@ -25,8 +26,8 @@
 
 
 def column_parts(half, n):
-    tiles = half // 128
-    cuts = [128 * (tiles * k // n) for k in range(n + 1)]
+    tiles = half // TILE
+    cuts = [TILE * (tiles * k // n) for k in range(n + 1)]
     return [(cuts[k], cuts[k + 1] - cuts[k]) for k in range(n)]
 
 
@@ -70,7 +71,7 @@
 
 def scatter_scratch(bits, half):
     shapes = [pltpu.VMEM((2,) * len(bits) + (16, half), BF16), pltpu.VMEM((2, 8, half), F32)]
-    shapes += [pltpu.VMEM((8, half), F32)]
+    shapes += [pltpu.VMEM((8, half), F32), pltpu.VMEM((2,) * len(bits) + (16, half), BF16)]
     orders = chain_orders(bits)
     for _, width in column_parts(half, len(orders)):
         for done in range(len(bits) + 1):
@@ -79,13 +80,13 @@
     return shapes + [pltpu.SemaphoreType.DMA((count,)), pltpu.SemaphoreType.DMA((count,))]
 
 
-def reduce_scatter(bits, place, half, x_ref, out_ref, scratch):
-    held, own, swapped = scratch[:3]
+def reduce_scatter(bits, place, half, left_ref, right_ref, out_ref, scratch):
+    held, own, swapped, leaving = scratch[:4]
     sems = scratch[-2:]
     orders = chain_orders(bits)
     parts = column_parts(half, len(orders))
     n = len(bits)
-    landed = [scratch[3 + k * (n + 1): 3 + (k + 1) * (n + 1)] for k in range(len(orders))]
+    landed = [scratch[4 + k * (n + 1): 4 + (k + 1) * (n + 1)] for k in range(len(orders))]
     every = (slice(None),) * (n + 1)
     core = place.core
     copies, now = [], []
@@ -95,21 +96,35 @@
         copies.append(copy)
         return copy
 
+    def product(offset, start, width, store):
+        def tile(i, carry):
+            at = pl.multiple_of(start + i * TILE, TILE)
+            right = right_ref[:, columns(offset + at, TILE)]
+            value = jnp.dot(left_ref[...], right, preferred_element_type=F32)
+            store(pl.ds(at, TILE), value)
+            return carry
+
+        lax.fori_loop(0, width // TILE, tile, 0)
+
+    def leave(here, value):
+        leaving[every + (here,)] = value.astype(BF16).reshape(leaving.shape[:-1] + (TILE,))
+
+    def stay(here, value):
+        held[every + (here,)] = value.astype(BF16).reshape(held.shape[:-1] + (TILE,))
+
     for k, (start, width) in enumerate(parts):
-        src = x_ref.at[every + (columns((1 - core) * half + start, width),)]
+        product((1 - core) * half, start, width, leave)
+        src = leaving.at[every + (pl.ds(start, width),)]
         now.append(launch(src, landed[k][0], sems, k * (n + 2), place.sibling))
+    for start, width in parts:
+        product(core * half, start, width, stay)
     for stage in range(n + 1):
         for k, (start, width) in enumerate(parts):
             here = pl.ds(start, width)
             now[k].wait_recv()
             done = orders[k][:stage]
             keep = tuple(place.mine[i] if i in done else slice(None) for i in range(n)) + (slice(None),)
-            base = (
-                x_ref[every + (columns(core * half + start, width),)]
-                if stage == 0
-                else held[keep + (here,)]
-            )
-            total = base.astype(F32) + landed[k][stage][...].astype(F32)
+            total = held[keep + (here,)].astype(F32) + landed[k][stage][...].astype(F32)
             if stage < n:
                 held[keep + (here,)] = total.astype(BF16)
                 bit = orders[k][stage]
@@ -136,16 +151,17 @@
 
 def gather_scratch(bits, half):
     orders = chain_orders(bits)
-    count = len(orders) * (len(bits) + 2)
+    count = (len(orders) + 1) * (len(bits) + 2)
     return [
         pltpu.VMEM((8, half), F32),
+        pltpu.VMEM((8, 128), F32),
         pltpu.SemaphoreType.DMA((count,)),
         pltpu.SemaphoreType.DMA((count,)),
     ]
 
 
-def gather(bits, place, half, rows_ref, out_ref, scratch):
-    swapped, sems = scratch[0], scratch[1:]
+def gather(bits, place, half, rows_ref, small_ref, out_ref, small_out, scratch):
+    swapped, small_swapped, sems = scratch[0], scratch[1], scratch[2:]
     orders = chain_orders(bits)
     parts = column_parts(half, len(orders))
     n = len(bits)
@@ -160,17 +176,32 @@
     for k, (start, width) in enumerate(parts):
         src = rows_ref.at[:, columns((1 - core) * half + start, width)]
         now.append(launch(src, swapped.at[:, pl.ds(start, width)], sems, k * (n + 2), place.sibling))
+    now.append(launch(small_ref, small_swapped, sems, len(parts) * (n + 2), place.sibling))
+
+    def chip_block(mine, other):
+        first = jnp.where(core == 0, mine, other)
+        second = jnp.where(core == 0, other, mine)
+        return jnp.concatenate([first, second], axis=0).astype(BF16)
+
+    own = tuple(place.mine) + (slice(None),)
     for stage in range(n + 1):
+        k = len(parts)
+        now[k].wait_recv()
+        order = orders[0][::-1]
+        if stage == 0:
+            small_out[own + (slice(None),)] = chip_block(small_ref[...], small_swapped[...])
+        if stage < n:
+            done = order[:stage]
+            at = tuple(slice(None) if i in done else place.mine[i] for i in range(n))
+            part = small_out.at[at + (slice(None), slice(None))]
+            now[k] = launch(part, part, sems, k * (n + 2) + stage + 1, place.partner[order[stage]])
         for k, (start, width) in enumerate(parts):
             here = columns(core * half + start, width)
             now[k].wait_recv()
             order = orders[k][::-1]
             if stage == 0:
-                mine, other = rows_ref[:, here], swapped[:, pl.ds(start, width)]
-                first = jnp.where(core == 0, mine, other)
-                second = jnp.where(core == 0, other, mine)
-                block = jnp.concatenate([first, second], axis=0).astype(BF16)
-                out_ref[tuple(place.mine) + (slice(None), here)] = block
+                block = chip_block(rows_ref[:, here], swapped[:, pl.ds(start, width)])
+                out_ref[own + (here,)] = block
             done = order[:stage]
             at = tuple(slice(None) if i in done else place.mine[i] for i in range(n))
             part = out_ref.at[at + (slice(None), here)]
@@ -182,69 +213,113 @@
         copy.wait_send()
 
 
-def middle_kernel(tp_bits, all_bits, x_ref, residual_ref, hidden_ref, rows_ref, normed, *scratch):
+def middle_kernel(
+    tp_bits, all_bits, values_ref, out_weight_ref, residual_ref, weights_ref,
+    hidden_ref, rows_ref, weights_out, normed, *scratch
+):
     half = residual_ref.shape[1] // 2
     place_all = Place(all_bits)
     place = Place(tp_bits)
     place_all.greet()
     cut = len(scatter_scratch(tp_bits, half))
-    reduce_scatter(tp_bits, place, half, x_ref, hidden_ref, scratch[:cut])
+    reduce_scatter(tp_bits, place, half, values_ref, out_weight_ref, hidden_ref, scratch[:cut])
     state = hidden_ref[...] + residual_ref[...].astype(F32)
     hidden_ref[...] = state
     normed[...] = state * lax.rsqrt(jnp.mean(state * state, axis=-1, keepdims=True) + 1e-06)
-    gather(all_bits, place_all, half, normed, rows_ref, scratch[cut:])
-
-
-def final_kernel(all_bits, x_ref, hidden_ref, out_ref, routed, *scratch):
+    gather(all_bits, place_all, half, normed, weights_ref, rows_ref, weights_out, scratch[cut:])
+
+
+def final_kernel(all_bits, inner_ref, w_down_ref, hidden_ref, out_ref, routed, *scratch):
     half = hidden_ref.shape[1] // 2
     place = Place(all_bits)
     place.greet()
-    reduce_scatter(all_bits, place, half, x_ref, routed, scratch)
+    reduce_scatter(all_bits, place, half, inner_ref, w_down_ref, routed, scratch)
     out_ref[...] = (routed[...] + hidden_ref[...]).astype(out_ref.dtype)
 
 
+def exchange_kernel(peers, x_ref, out_ref, send_sems, recv_sems, own_sem):
+    g, t = lax.axis_index("grp"), lax.axis_index("tp")
+    shifts = sorted(range(1, peers), key=lambda d: (abs(d - peers // 2), d))
+    barrier = pltpu.get_barrier_semaphore()
+    for d in shifts:
+        pl.semaphore_signal(
+            barrier, inc=1, device_id=(g, (t + d) % peers), device_id_type=MESH
+        )
+    pl.semaphore_wait(barrier, peers - 1)
+    copies = []
+    for d in shifts:
+        to = (t + d) % peers
+        copies.append(send(x_ref.at[to], out_ref.at[t], (send_sems, recv_sems), d, (g, to)))
+    own = pltpu.make_async_copy(x_ref.at[t], out_ref.at[t], own_sem)
+    own.start()
+    own.wait()
+    for copy in copies:
+        copy.wait_recv()
+    for copy in copies:
+        copy.wait_send()
+
+
 VMEM = pl.BlockSpec(memory_space=pltpu.VMEM)
 
 
-def middle(part, residual, groups, peers):
+def exchange(blocks, peers):
+    return pl.pallas_call(
+        functools.partial(exchange_kernel, peers),
+        out_shape=jax.ShapeDtypeStruct(blocks.shape, blocks.dtype),
+        in_specs=[VMEM],
+        out_specs=VMEM,
+        scratch_shapes=[
+            pltpu.SemaphoreType.DMA((peers,)),
+            pltpu.SemaphoreType.DMA((peers,)),
+            pltpu.SemaphoreType.DMA(()),
+        ],
+        compiler_params=pltpu.CompilerParams(
+            collective_id=2, has_side_effects=True, vmem_limit_bytes=8 << 20
+        ),
+    )(blocks)
+
+
+def middle(values, out_weight, residual, weights, groups, peers):
     width = residual.shape[1]
     grp_bits, tp_bits = axis_bits(groups, peers)
     both = grp_bits + tp_bits
     rows = groups * peers * 8
-    need = width * 2 * (3 * part.shape[0] + rows) + (12 << 20)
-    hidden, gathered = pl.pallas_call(
+    need = width * 2 * (3 * values.shape[0] + rows + values.shape[1]) + (12 << 20)
+    shape = (2,) * len(both) + (16,)
+    hidden, gathered, weights_all = pl.pallas_call(
         functools.partial(middle_kernel, tp_bits, both),
         out_shape=(
             jax.ShapeDtypeStruct((8, width), F32),
-            jax.ShapeDtypeStruct((2,) * len(both) + (16, width), BF16),
+            jax.ShapeDtypeStruct(shape + (width,), BF16),
+            jax.ShapeDtypeStruct(shape + (128,), BF16),
         ),
-        in_specs=[VMEM, VMEM],
-        out_specs=(VMEM, VMEM),
+        in_specs=[VMEM] * 4,
+        out_specs=(VMEM,) * 3,
         scratch_shapes=[pltpu.VMEM((8, width), F32)]
         + scatter_scratch(tp_bits, width // 2)
         + gather_scratch(both, width // 2),
         compiler_params=pltpu.CompilerParams(
             collective_id=0, has_side_effects=True, vmem_limit_bytes=need
         ),
-    )(part.reshape((2,) * len(tp_bits) + (16, width)), residual)
-    return hidden, gathered.reshape(rows, width)
-
-
-def final(part, hidden, groups, peers):
+    )(values, out_weight, residual, weights)
+    return hidden, gathered.reshape(rows, width), weights_all.reshape(rows, 128)
+
+
+def final(inner, w_down, hidden, groups, peers):
     width = hidden.shape[1]
     grp_bits, tp_bits = axis_bits(groups, peers)
     both = grp_bits + tp_bits
-    need = width * 2 * 3 * part.shape[0] + (12 << 20)
+    need = width * 2 * (2 * inner.shape[0] + inner.shape[1]) + (12 << 20)
     return pl.pallas_call(
         functools.partial(final_kernel, both),
         out_shape=jax.ShapeDtypeStruct((8, width), BF16),
-        in_specs=[VMEM, VMEM],
+        in_specs=[VMEM] * 3,
         out_specs=VMEM,
         scratch_shapes=[pltpu.VMEM((8, width), F32)] + scatter_scratch(both, width // 2),
         compiler_params=pltpu.CompilerParams(
             collective_id=1, has_side_effects=True, vmem_limit_bytes=need
         ),
-    )(part.reshape((2,) * len(both) + (16, width)), hidden)
+    )(inner, w_down, hidden)
 
 
 def body(
@@ -262,7 +337,6 @@
 ):
     rows_here = residual.shape[0]
     latent = uv_weight.shape[1]
-    width = residual.shape[1]
     span = kv_cache.shape[1]
     scores = jnp.einsum(
         "rhc,rlc->rhl", queries, kv_cache, preferred_element_type=jnp.float32
@@ -274,30 +348,29 @@
     context = jnp.einsum(
         "rhl,rlc->rhc", probs, kv_cache[:, :, :latent], preferred_element_type=jnp.float32
     ).astype(jnp.bfloat16)
-    grouped = lax.all_to_all(context, "tp", split_axis=1, concat_axis=0, tiled=True)
+    groups, peers = lax.axis_size("grp"), lax.axis_size("tp")
+    heads_here = uv_weight.shape[0]
+    blocks = context.transpose(1, 0, 2).reshape(peers, heads_here * rows_here, latent)
+    grouped = exchange(blocks, peers).reshape(peers, heads_here, rows_here, latent)
     values = jnp.einsum(
-        "rhc,hcv->rhv", grouped, uv_weight, preferred_element_type=jnp.float32
+        "phrc,hcv->prhv", grouped, uv_weight, preferred_element_type=jnp.float32
     ).astype(jnp.bfloat16)
-    values = values.reshape(values.shape[0], values.shape[1] * values.shape[2])
-    groups, peers = lax.axis_size("grp"), lax.axis_size("tp")
-    attention = jnp.dot(values, out_weight, preferred_element_type=jnp.float32).astype(BF16)
-    hidden_state, rows_all = middle(attention, residual, groups, peers)
-    experts = lax.axis_size("tp")
-    me = lax.axis_index("tp")
-    ids_hot = expert_ids[:, :, None] == lax.broadcasted_iota(jnp.int32, (1, 1, experts), 2)
+    values = values.reshape(peers * rows_here, heads_here * values.shape[3])
+    ids_hot = expert_ids[:, :, None] == lax.broadcasted_iota(jnp.int32, (1, 1, 128), 2)
     weights = jnp.sum(
         jnp.where(ids_hot, gate_values.astype(jnp.float32)[:, :, None], 0.0), axis=1
-    ).astype(jnp.bfloat16)
-    weights_all = lax.all_gather(weights, ("grp", "tp"), axis=0, tiled=True)
-    own = lax.broadcasted_iota(jnp.int32, (1, experts), 1) == me
+    )
+    hidden_state, rows_all, weights_all = middle(
+        values, out_weight, residual, weights, groups, peers
+    )
+    own = lax.broadcasted_iota(jnp.int32, (1, 128), 1) == lax.axis_index("tp")
     weight = jnp.sum(
         jnp.where(own, weights_all.astype(jnp.float32), 0.0), axis=1, keepdims=True
     )
     gate = jnp.dot(rows_all, w_gate[0], preferred_element_type=jnp.float32)
     up = jnp.dot(rows_all, w_up[0], preferred_element_type=jnp.float32)
-    hidden = (jax.nn.silu(gate) * up * weight).astype(jnp.bfloat16)
-    partial_value = jnp.dot(hidden, w_down[0], preferred_element_type=jnp.float32)
-    return final(partial_value.astype(jnp.bfloat16), hidden_state, groups, peers)
+    inner = (jax.nn.silu(gate) * up * weight).astype(jnp.bfloat16)
+    return final(inner, w_down[0], hidden_state, groups, peers)
 
 
 def solution(mesh):

time: 172 us -> 143 us (0.83)
  blocking collectives: 52.9 us -> 0 us
  Pallas kernels: 75 us -> 114 us
  matrix products: 28.9 us -> 15.6 us
  starting transfers between devices: 7.39 us -> 0 us
  local copies, waits for them, and re-layouts: 6.53 us -> 10.2 us
    all_gather x1 -> x0, blocking collectives: 52.9 us -> none  [body(): weights_all = lax.all_gather(weights, ('grp', 'tp'), axis=0, tiled=True)]
    pallas_call x0 -> x1, Pallas kernels: none -> 27.8 us  [exchange(): pl.pallas_call(functools.partial(exchange_kernel, peers), out_shape=jax.S...]
    dot_general x3 -> x2, matrix products: 18 us -> 1.54 us  [the longest x1 1.11 us: body(): up = jnp.dot(rows_all, w_up[0], preferred_element_type=jnp.float32)]
    pallas_call x1, Pallas kernels: 47.2 us -> 54.9 us  [middle(): pl.pallas_call(functools.partial(middle_kernel, tp_bits, both), out_shape...]
    all_to_all x1 -> x0, starting transfers between devices: 7.39 us -> none  [body(): lax.all_to_all(context, 'tp', split_axis=1, concat_axis=0, tiled=True)]
    unnamed x17, local copies, waits for them, and re-layouts: 4.96 us -> 9.43 us
    pallas_call x1, Pallas kernels: 27.8 us -> 31.7 us  [final(): pl.pallas_call(functools.partial(final_kernel, both), out_shape=jax.Shape...]
    dot_general x1, matrix products: 1.18 us -> 4.4 us  [body(): gate = jnp.dot(rows_all, w_gate[0], preferred_element_type=jnp.float32)]
  transfers between devices with their start and end apart: 1 -> 0, of which waited for: 0 -> 0; matrix products, arithmetic and copies ran while one was open for 0% -> 0% of each run, Pallas kernels for 0% -> 0%
where the time goes in v3:
time: 143 us
  Pallas kernels  114 us (80%)
  matrix products  15.6 us (11%)
  local copies, waits for them, and re-layouts  10.2 us (7%)
  other arithmetic  2.4 us (2%)
    pallas_call x1, Pallas kernels, middle(): pl.pallas_call(functools.partial(middle_kernel, tp_bits, both), out_shape...  54.9 us
    pallas_call x1, Pallas kernels, final(): pl.pallas_call(functools.partial(final_kernel, both), out_shape=jax.Shape...  31.7 us
    pallas_call x1, Pallas kernels, exchange(): pl.pallas_call(functools.partial(exchange_kernel, peers), out_shape=jax.S...  27.8 us
    unnamed x17, local copies, waits for them, and re-layouts  9.43 us
    sub x1, matrix products, body(): expo = jnp.where(valid, jnp.exp(scores - top), 0.0)  5.97 us
    dot_general x1, matrix products, body(): gate = jnp.dot(rows_all, w_gate[0], preferred_element_type=jnp.float32)  4.4 us
    dot_general x1, matrix products, body(): jnp.einsum('rhl,rlc->rhc', probs, kv_cache[:, :, :latent], preferred_elem...  3.74 us

profile of v3, /device:TPU:0, one launch (start us, length us, event | category | flops | bytes accessed | tf_op | source)
XLA Modules:
  0.0 142.8 jit_solution(3072572653063645590)
XLA Ops:
  0.0 0.8 iota_compare_fusion.1
  0.8 0.7 convert_element_type.31
  1.5 0.8 select_reduce_fusion.2.weights_ref
  2.3 6.0 %fusion.35 = (f32[8,128]{1,0:T(8,128)S(1)}, f32[8,128,512]{2,1,0:T(8,128)S(1)}) fusion(pred[8,512]{1,0:T(8,128)(4,1)S(1)} %iota_compare_fusion.1, bf16[8,128,576]{1,2,0:T(8,128)(2,1)S(1)} %copy-done, bf16[8,512,576]{1,2,0:T(8,128)(2,1)} %param.12), kind=kOutput, calls=%fused_computation.33 | convolution fusion | flops 1211105792 | bytes 8003584 | tf_op jit(solution)/shard_map/sub | solution.py:346
  8.3 3.7 %fusion.14 = bf16[128,8,512]{2,0,1:T(8,128)(2,1)S(1)} fusion(bf16[8,512,576]{1,2,0:T(8,128)(2,1)} %param.12, f32[8,128,512]{2,1,0:T(8,128)S(1)} %get-tuple-element.12, f32[8,128]{1,0:T(8,128)S(1)} %get-tuple-element.11), kind=kOutput, calls=%fused_computation.13 | convolution fusion | flops 538443776 | bytes 7344128 | tf_op jit(solution)/shard_map/rhl,rlc->rhc/dot_general | solution.py:348
  12.0 0.0 copy-start.6
  12.0 0.0 copy-start.3
  12.0 0.6 copy.17
  12.6 27.8 %shard_map.109 = bf16[16,64,512]{2,1,0:T(8,128)(2,1)S(1)} custom-call(bf16[16,64,512]{2,1,0:T(8,128)(2,1)S(1)} %bitcast.37), custom_call_target="tpu_custom_call" | custom-call | tf_op jit(solution)/shard_map/pallas_call | solution.py:266
  40.5 0.4 fusion.23
  40.9 0.1 copy.25
  41.0 0.0 copy-start.1
  41.0 5.2 %copy-done.1 = bf16[1024,7168]{1,0:T(8,128)(2,1)S(1)} copy-done((bf16[1024,7168]{1,0:T(8,128)(2,1)S(1)}, bf16[1024,7168]{1,0:T(8,128)(2,1)}, u32[]{:S(2)}) %copy-start.1) | copy-done | bytes 14680088
  46.2 54.9 %shard_map.110 = (f32[8,7168]{1,0:T(8,128)S(1)}, bf16[2,2,2,2,16,7168]{5,4,3,2,1,0:T(8,128)(2,1)S(1)}, bf16[2,2,2,2,16,128]{5,4,3,2,1,0:T(8,128)(2,1)S(1)}) custom-call(bf16[128,1024]{1,0:T(8,128)(2,1)S(1)} %bitcast.39, bf16[1024,7168]{1,0:T(8,128)(2,1)S(1)} %copy-done.1, bf16[8,7168]{1,0:T(8,128)(2,1)S(1)} %copy-done.3, ...), custom_call_target="tpu_custom_call" | custom-call | tf_op jit(solution)/shard_map/pallas_call | solution.py:289
  101.1 1.8 %copy-done.4 = bf16[2,2,2,2,16,7168]{5,4,3,2,1,0:T(8,128)(2,1)} copy-done((bf16[2,2,2,2,16,7168]{5,4,3,2,1,0:T(8,128)(2,1)}, bf16[2,2,2,2,16,7168]{5,4,3,2,1,0:T(8,128)(2,1)S(1)}, u32[]{:S(2)}) %copy-start.4) | copy-done | bytes 3670040
  102.9 0.1 select_reduce_fusion.1
  103.0 0.1 mul.27
  103.1 0.0 copy-start.7
  103.1 4.4 %fusion.5 = f32[256,256]{1,0:T(8,128)S(1)} fusion(bf16[256,7168]{1,0:T(8,128)(2,1)} %bitcast.40, bf16[1,7168,256]{2,1,0:T(8,128)(2,1)} %param.19), kind=kOutput, calls=%fused_computation.5 | convolution fusion | flops 939524096 | bytes 7602176 | tf_op jit(solution)/shard_map/dot_general | solution.py:370
  107.6 0.9 copy-done.7
  108.4 1.1 fusion.24.inner_ref
  109.6 0.9 copy-done.2
  110.5 31.7 %shard_map.111 = bf16[8,7168]{1,0:T(8,128)(2,1)S(1)} custom-call(bf16[256,256]{1,0:T(8,128)(2,1)S(1)} %fusion.24.inner_ref, bf16[256,7168]{1,0:T(8,128)(2,1)S(1)} %bitcast.38, f32[8,7168]{1,0:T(8,128)S(1)} %get-tuple-element.10.hidden_ref), custom_call_target="tpu_custom_call" | custom-call | tf_op jit(solution)/shard_map/pallas_call | solution.py:313
  142.2 0.6 copy.27
  (9 shorter events, 0.0 us)
Async XLA Ops:
  0.0 2.3 %copy-start = (bf16[8,128,576]{1,2,0:T(8,128)(2,1)S(1)}, bf16[8,128,576]{1,2,0:T(8,128)(2,1)}, u32[]{:S(2)}) copy-start(bf16[8,128,576]{1,2,0:T(8,128)(2,1)} %param.11) | copy-start | bytes 3538948
  12.0 28.5 %copy-start.6 = (bf16[8,512,128]{2,1,0:T(8,128)(2,1)S(1)}, bf16[8,512,128]{2,1,0:T(8,128)(2,1)}, u32[]{:S(2)}) copy-start(bf16[8,512,128]{2,1,0:T(8,128)(2,1)} %param.15) | copy-start | bytes 3145732
  12.0 29.0 %copy-start.3 = (bf16[8,7168]{1,0:T(8,128)(2,1)S(1)}, bf16[8,7168]{1,0:T(8,128)(2,1)}, u32[]{:S(2)}) copy-start(bf16[8,7168]{1,0:T(8,128)(2,1)} %residual_ref.1) | copy-start | bytes 344068
  41.0 5.2 %copy-start.1 = (bf16[1024,7168]{1,0:T(8,128)(2,1)S(1)}, bf16[1024,7168]{1,0:T(8,128)(2,1)}, u32[]{:S(2)}) copy-start(bf16[1024,7168]{1,0:T(8,128)(2,1)} %out_weight_ref.1) | copy-start | bytes 44040196
  101.1 1.8 %copy-start.4 = (bf16[2,2,2,2,16,7168]{5,4,3,2,1,0:T(8,128)(2,1)}, bf16[2,2,2,2,16,7168]{5,4,3,2,1,0:T(8,128)(2,1)S(1)}, u32[]{:S(2)}) copy-start(bf16[2,2,2,2,16,7168]{5,4,3,2,1,0:T(8,128)(2,1)S(1)} %get-tuple-element.8) | copy-start | bytes 11010052
  103.1 4.4 %copy-start.5 = (bf16[2,2,2,2,16,7168]{5,4,3,2,1,0:T(8,128)(2,1)S(1)}, bf16[2,2,2,2,16,7168]{5,4,3,2,1,0:T(8,128)(2,1)}, u32[]{:S(2)}) copy-start(bf16[2,2,2,2,16,7168]{5,4,3,2,1,0:T(8,128)(2,1)} %copy-done.4) | copy-start | bytes 11010052
  103.1 5.3 %copy-start.7 = (bf16[1,7168,256]{2,1,0:T(8,128)(2,1)S(1)}, bf16[1,7168,256]{2,1,0:T(8,128)(2,1)}, u32[]{:S(2)}) copy-start(bf16[1,7168,256]{2,1,0:T(8,128)(2,1)} %param.20) | copy-start | bytes 11010052
  108.4 2.0 %copy-start.2 = (bf16[1,256,7168]{2,1,0:T(8,128)(2,1)S(1)}, bf16[1,256,7168]{2,1,0:T(8,128)(2,1)}, u32[]{:S(2)}) copy-start(bf16[1,256,7168]{2,1,0:T(8,128)(2,1)} %param.21) | copy-start | bytes 11010052

commit v4 on v3

--- a/solution.py
+++ b/solution.py
@@ -80,7 +80,12 @@
     return shapes + [pltpu.SemaphoreType.DMA((count,)), pltpu.SemaphoreType.DMA((count,))]
 
 
-def reduce_scatter(bits, place, half, left_ref, right_ref, out_ref, scratch):
+def right_scratch(right, bits):
+    count = 2 * len(chain_orders(bits))
+    return [pltpu.VMEM(right.shape, right.dtype), pltpu.SemaphoreType.DMA((count,))]
+
+
+def reduce_scatter(bits, place, half, left_ref, right_ref, right, fetched, out_ref, scratch):
     held, own, swapped, leaving = scratch[:4]
     sems = scratch[-2:]
     orders = chain_orders(bits)
@@ -96,11 +101,24 @@
         copies.append(copy)
         return copy
 
+    loads = []
+
+    def fetch(offset, start, width):
+        at = (slice(None), columns(offset + start, width))
+        load = pltpu.make_async_copy(right_ref.at[at], right.at[at], fetched.at[len(loads)])
+        load.start()
+        loads.append(load)
+
+    for start, width in parts:
+        fetch((1 - core) * half, start, width)
+    for start, width in parts:
+        fetch(core * half, start, width)
+
     def product(offset, start, width, store):
         def tile(i, carry):
             at = pl.multiple_of(start + i * TILE, TILE)
-            right = right_ref[:, columns(offset + at, TILE)]
-            value = jnp.dot(left_ref[...], right, preferred_element_type=F32)
+            weight = right[:, columns(offset + at, TILE)]
+            value = jnp.dot(left_ref[...], weight, preferred_element_type=F32)
             store(pl.ds(at, TILE), value)
             return carry
 
@@ -113,10 +131,12 @@
         held[every + (here,)] = value.astype(BF16).reshape(held.shape[:-1] + (TILE,))
 
     for k, (start, width) in enumerate(parts):
+        loads[k].wait()
         product((1 - core) * half, start, width, leave)
         src = leaving.at[every + (pl.ds(start, width),)]
         now.append(launch(src, landed[k][0], sems, k * (n + 2), place.sibling))
-    for start, width in parts:
+    for k, (start, width) in enumerate(parts):
+        loads[len(parts) + k].wait()
         product(core * half, start, width, stay)
     for stage in range(n + 1):
         for k, (start, width) in enumerate(parts):
@@ -215,25 +235,25 @@
 
 def middle_kernel(
     tp_bits, all_bits, values_ref, out_weight_ref, residual_ref, weights_ref,
-    hidden_ref, rows_ref, weights_out, normed, *scratch
+    hidden_ref, rows_ref, weights_out, right, fetched, normed, *scratch
 ):
     half = residual_ref.shape[1] // 2
     place_all = Place(all_bits)
     place = Place(tp_bits)
     place_all.greet()
     cut = len(scatter_scratch(tp_bits, half))
-    reduce_scatter(tp_bits, place, half, values_ref, out_weight_ref, hidden_ref, scratch[:cut])
+    reduce_scatter(tp_bits, place, half, values_ref, out_weight_ref, right, fetched, hidden_ref, scratch[:cut])
     state = hidden_ref[...] + residual_ref[...].astype(F32)
     hidden_ref[...] = state
     normed[...] = state * lax.rsqrt(jnp.mean(state * state, axis=-1, keepdims=True) + 1e-06)
     gather(all_bits, place_all, half, normed, weights_ref, rows_ref, weights_out, scratch[cut:])
 
 
-def final_kernel(all_bits, inner_ref, w_down_ref, hidden_ref, out_ref, routed, *scratch):
+def final_kernel(all_bits, inner_ref, w_down_ref, hidden_ref, out_ref, right, fetched, routed, *scratch):
     half = hidden_ref.shape[1] // 2
     place = Place(all_bits)
     place.greet()
-    reduce_scatter(all_bits, place, half, inner_ref, w_down_ref, routed, scratch)
+    reduce_scatter(all_bits, place, half, inner_ref, w_down_ref, right, fetched, routed, scratch)
     out_ref[...] = (routed[...] + hidden_ref[...]).astype(out_ref.dtype)
 
 
@@ -260,6 +280,7 @@
 
 
 VMEM = pl.BlockSpec(memory_space=pltpu.VMEM)
+ANY = pl.BlockSpec(memory_space=pl.ANY)
 
 
 def exchange(blocks, peers):
@@ -293,9 +314,10 @@
             jax.ShapeDtypeStruct(shape + (width,), BF16),
             jax.ShapeDtypeStruct(shape + (128,), BF16),
         ),
-        in_specs=[VMEM] * 4,
+        in_specs=[VMEM, ANY, VMEM, VMEM],
         out_specs=(VMEM,) * 3,
-        scratch_shapes=[pltpu.VMEM((8, width), F32)]
+        scratch_shapes=right_scratch(out_weight, tp_bits)
+        + [pltpu.VMEM((8, width), F32)]
         + scatter_scratch(tp_bits, width // 2)
         + gather_scratch(both, width // 2),
         compiler_params=pltpu.CompilerParams(
@@ -313,9 +335,11 @@
     return pl.pallas_call(
         functools.partial(final_kernel, both),
         out_shape=jax.ShapeDtypeStruct((8, width), BF16),
-        in_specs=[VMEM] * 3,
+        in_specs=[VMEM, ANY, VMEM],
         out_specs=VMEM,
-        scratch_shapes=[pltpu.VMEM((8, width), F32)] + scatter_scratch(both, width // 2),
+        scratch_shapes=right_scratch(w_down, both)
+        + [pltpu.VMEM((8, width), F32)]
+        + scatter_scratch(both, width // 2),
         compiler_params=pltpu.CompilerParams(
             collective_id=1, has_side_effects=True, vmem_limit_bytes=need
         ),

time: 143 us -> 145 us (1.014)
  Pallas kernels: 114 us -> 117 us
    pallas_call x1, Pallas kernels: 54.9 us -> 56.9 us  [middle(): pl.pallas_call(functools.partial(middle_kernel, tp_bits, both), out_shape...]
where the time goes in v4:
time: 145 us
  Pallas kernels  117 us (81%)
  matrix products  15.6 us (11%)
  local copies, waits for them, and re-layouts  10.2 us (7%)
  other arithmetic  2.4 us (2%)
    pallas_call x1, Pallas kernels, middle(): pl.pallas_call(functools.partial(middle_kernel, tp_bits, both), out_shape...  56.9 us
    pallas_call x1, Pallas kernels, final(): pl.pallas_call(functools.partial(final_kernel, both), out_shape=jax.Shape...  32 us
    pallas_call x1, Pallas kernels, exchange(): pl.pallas_call(functools.partial(exchange_kernel, peers), out_shape=jax.S...  27.8 us
    unnamed x17, local copies, waits for them, and re-layouts  9.43 us
    sub x1, matrix products, body(): expo = jnp.where(valid, jnp.exp(scores - top), 0.0)  5.97 us
    dot_general x1, matrix products, body(): gate = jnp.dot(rows_all, w_gate[0], preferred_element_type=jnp.float32)  4.4 us
    dot_general x1, matrix products, body(): jnp.einsum('rhl,rlc->rhc', probs, kv_cache[:, :, :latent], preferred_elem...  3.74 us

profile of v4, /device:TPU:0, one launch (start us, length us, event | category | flops | bytes accessed | tf_op | source)
XLA Modules:
  0.0 145.1 jit_solution(8263738400206887933)
XLA Ops:
  0.0 0.8 iota_compare_fusion.1
  0.8 0.7 convert_element_type.31
  1.5 0.8 select_reduce_fusion.2.weights_ref
  2.3 6.0 %fusion.35 = (f32[8,128]{1,0:T(8,128)S(1)}, f32[8,128,512]{2,1,0:T(8,128)S(1)}) fusion(pred[8,512]{1,0:T(8,128)(4,1)S(1)} %iota_compare_fusion.1, bf16[8,128,576]{1,2,0:T(8,128)(2,1)S(1)} %copy-done, bf16[8,512,576]{1,2,0:T(8,128)(2,1)} %param.12), kind=kOutput, calls=%fused_computation.33 | convolution fusion | flops 1211105792 | bytes 8003584 | tf_op jit(solution)/shard_map/sub | solution.py:370
  8.3 3.7 %fusion.14 = bf16[128,8,512]{2,0,1:T(8,128)(2,1)S(1)} fusion(bf16[8,512,576]{1,2,0:T(8,128)(2,1)} %param.12, f32[8,128,512]{2,1,0:T(8,128)S(1)} %get-tuple-element.12, f32[8,128]{1,0:T(8,128)S(1)} %get-tuple-element.11), kind=kOutput, calls=%fused_computation.13 | convolution fusion | flops 538443776 | bytes 7344128 | tf_op jit(solution)/shard_map/rhl,rlc->rhc/dot_general | solution.py:372
  12.0 0.0 copy-start.6
  12.0 0.0 copy-start.3
  12.0 0.6 copy.17
  12.6 27.8 %shard_map.109 = bf16[16,64,512]{2,1,0:T(8,128)(2,1)S(1)} custom-call(bf16[16,64,512]{2,1,0:T(8,128)(2,1)S(1)} %bitcast.37), custom_call_target="tpu_custom_call" | custom-call | tf_op jit(solution)/shard_map/pallas_call | solution.py:287
  40.5 0.4 fusion.23
  40.9 0.1 copy.25
  41.0 0.0 copy-start.1
  41.0 5.2 %copy-done.1 = bf16[1024,7168]{1,0:T(8,128)(2,1)S(1)} copy-done((bf16[1024,7168]{1,0:T(8,128)(2,1)S(1)}, bf16[1024,7168]{1,0:T(8,128)(2,1)}, u32[]{:S(2)}) %copy-start.1) | copy-done | bytes 14680088
  46.2 56.9 %shard_map.110 = (f32[8,7168]{1,0:T(8,128)S(1)}, bf16[2,2,2,2,16,7168]{5,4,3,2,1,0:T(8,128)(2,1)S(1)}, bf16[2,2,2,2,16,128]{5,4,3,2,1,0:T(8,128)(2,1)S(1)}) custom-call(bf16[128,1024]{1,0:T(8,128)(2,1)S(1)} %bitcast.39, bf16[1024,7168]{1,0:T(8,128)(2,1)S(1)} %copy-done.1, bf16[8,7168]{1,0:T(8,128)(2,1)S(1)} %copy-done.3, ...), custom_call_target="tpu_custom_call" | custom-call | tf_op jit(solution)/shard_map/pallas_call | solution.py:310
  103.1 1.8 %copy-done.4 = bf16[2,2,2,2,16,7168]{5,4,3,2,1,0:T(8,128)(2,1)} copy-done((bf16[2,2,2,2,16,7168]{5,4,3,2,1,0:T(8,128)(2,1)}, bf16[2,2,2,2,16,7168]{5,4,3,2,1,0:T(8,128)(2,1)S(1)}, u32[]{:S(2)}) %copy-start.4) | copy-done | bytes 3670040
  104.9 0.1 select_reduce_fusion.1
  105.0 0.1 mul.27
  105.1 0.0 copy-start.7
  105.1 4.4 %fusion.5 = f32[256,256]{1,0:T(8,128)S(1)} fusion(bf16[256,7168]{1,0:T(8,128)(2,1)} %bitcast.40, bf16[1,7168,256]{2,1,0:T(8,128)(2,1)} %param.19), kind=kOutput, calls=%fused_computation.5 | convolution fusion | flops 939524096 | bytes 7602176 | tf_op jit(solution)/shard_map/dot_general | solution.py:394
  109.5 0.9 copy-done.7
  110.4 1.1 fusion.24.inner_ref
  111.5 0.9 copy-done.2
  112.5 32.0 %shard_map.111 = bf16[8,7168]{1,0:T(8,128)(2,1)S(1)} custom-call(bf16[256,256]{1,0:T(8,128)(2,1)S(1)} %fusion.24.inner_ref, bf16[256,7168]{1,0:T(8,128)(2,1)S(1)} %bitcast.38, f32[8,7168]{1,0:T(8,128)S(1)} %get-tuple-element.10.hidden_ref), custom_call_target="tpu_custom_call" | custom-call | tf_op jit(solution)/shard_map/pallas_call | solution.py:335
  144.5 0.6 copy.27
  (9 shorter events, 0.0 us)
Async XLA Ops:
  0.0 2.3 %copy-start = (bf16[8,128,576]{1,2,0:T(8,128)(2,1)S(1)}, bf16[8,128,576]{1,2,0:T(8,128)(2,1)}, u32[]{:S(2)}) copy-start(bf16[8,128,576]{1,2,0:T(8,128)(2,1)} %param.11) | copy-start | bytes 3538948
  12.0 28.5 %copy-start.6 = (bf16[8,512,128]{2,1,0:T(8,128)(2,1)S(1)}, bf16[8,512,128]{2,1,0:T(8,128)(2,1)}, u32[]{:S(2)}) copy-start(bf16[8,512,128]{2,1,0:T(8,128)(2,1)} %param.15) | copy-start | bytes 3145732
  12.0 29.0 %copy-start.3 = (bf16[8,7168]{1,0:T(8,128)(2,1)S(1)}, bf16[8,7168]{1,0:T(8,128)(2,1)}, u32[]{:S(2)}) copy-start(bf16[8,7168]{1,0:T(8,128)(2,1)} %residual_ref.1) | copy-start | bytes 344068
  41.0 5.2 %copy-start.1 = (bf16[1024,7168]{1,0:T(8,128)(2,1)S(1)}, bf16[1024,7168]{1,0:T(8,128)(2,1)}, u32[]{:S(2)}) copy-start(bf16[1024,7168]{1,0:T(8,128)(2,1)} %out_weight_ref.1) | copy-start | bytes 44040196
  103.1 1.8 %copy-start.4 = (bf16[2,2,2,2,16,7168]{5,4,3,2,1,0:T(8,128)(2,1)}, bf16[2,2,2,2,16,7168]{5,4,3,2,1,0:T(8,128)(2,1)S(1)}, u32[]{:S(2)}) copy-start(bf16[2,2,2,2,16,7168]{5,4,3,2,1,0:T(8,128)(2,1)S(1)} %get-tuple-element.8) | copy-start | bytes 11010052
  105.1 4.4 %copy-start.5 = (bf16[2,2,2,2,16,7168]{5,4,3,2,1,0:T(8,128)(2,1)S(1)}, bf16[2,2,2,2,16,7168]{5,4,3,2,1,0:T(8,128)(2,1)}, u32[]{:S(2)}) copy-start(bf16[2,2,2,2,16,7168]{5,4,3,2,1,0:T(8,128)(2,1)} %copy-done.4) | copy-start | bytes 11010052
  105.1 5.3 %copy-start.7 = (bf16[1,7168,256]{2,1,0:T(8,128)(2,1)S(1)}, bf16[1,7168,256]{2,1,0:T(8,128)(2,1)}, u32[]{:S(2)}) copy-start(bf16[1,7168,256]{2,1,0:T(8,128)(2,1)} %param.20) | copy-start | bytes 11010052
  110.4 2.0 %copy-start.2 = (bf16[1,256,7168]{2,1,0:T(8,128)(2,1)S(1)}, bf16[1,256,7168]{2,1,0:T(8,128)(2,1)}, u32[]{:S(2)}) copy-start(bf16[1,256,7168]{2,1,0:T(8,128)(2,1)} %param.21) | copy-start | bytes 11010052
